TPU v7x, 32 devices: a whole 2x2x4 slice. The times are simulated.
32 devices in a mesh: groups: 2 (over x), ctx: 16 (over z, y, core).
Axes of the slice: x: 2, y: 2, z: 4, core: 2. Of those that a mesh axis runs over, the one named last changes fastest.
Arguments:
- queries: bfloat16 [2048, 4096], P(('groups', 'ctx')), parts along dimension 0, may hold values from -256 to 256
- text_keys: bfloat16 [2048, 512], P(('groups', 'ctx')), parts along dimension 0, may hold values from -4 to 4
- text_values: bfloat16 [2048, 512], P(('groups', 'ctx')), parts along dimension 0, may hold values from -5 to 5
- image_features: bfloat16 [16384, 256], P(('groups', 'ctx')), parts along dimension 0, may hold values from -300 to 300
- kv_weight: bfloat16 [8192, 1024], P('ctx'), may hold values from -0.0625 to 0.0625
- image_grids: int32 [32, 3], P(('groups', 'ctx')), parts along dimension 0, may hold values from 0 to 58, as said below
Outputs:
- attention: bfloat16 [2048, 4096], P(('groups', 'ctx')), parts along dimension 0
- cache_keys: bfloat16 [2048, 512], P(('groups', 'ctx')), parts along dimension 0
- cache_values: bfloat16 [2048, 512], P(('groups', 'ctx')), parts along dimension 0
There are 2 independent parts, one for each index of `groups`. A program takes and returns all parts, laid end to end along the dimension named above; an argument that names none is the same for every part. Nothing has to cross between parts.
Inputs may be any that keep to these rules, and one draw needn't show every extreme that they name: `image_grids`: row b describes the one image of context shard b: offset o, grid rows gh and grid columns gw with 2 <= gh, gw <= 4; its tokens take positions b * 64 + o to b * 64 + o + gh * gw - 1, token k at grid row k // gw and column k % gw; o + gh * gw <= 62; some shard has a 4 x 4 image.
All inputs are finite; a program needn't handle non-finite values.
Results may differ from a plain program's by a relative error of at most 0.0053.
Values may be sent and summed in bfloat16 or wider, within the bound.
A program may use at most 128 MiB of HBM per device.

v0:
```python
import math

import jax
import jax.numpy as jnp
from jax import lax
from jax.sharding import PartitionSpec as P

D = 8192
HEAD_DIM = 128
GRID = 4


def rope_tables(time_ids, height_ids, width_ids):
    half_dim = HEAD_DIM // 2
    first_bound = HEAD_DIM // 8
    second_bound = first_bound + 3 * HEAD_DIM // 16
    pair_index = jnp.arange(half_dim, dtype=jnp.int32)
    inv_freq = 1000000.0 ** (-(2.0 * pair_index.astype(jnp.float32)) / HEAD_DIM)
    chosen = jnp.where(
        pair_index[None, :] < first_bound,
        time_ids[:, None],
        jnp.where(pair_index[None, :] < second_bound, height_ids[:, None], width_ids[:, None]),
    )
    angles = chosen.astype(jnp.float32) * inv_freq[None, :]
    cosine = jnp.concatenate([jnp.cos(angles), jnp.cos(angles)], axis=1)
    sine_table = jnp.concatenate([jnp.sin(angles), jnp.sin(angles)], axis=1)
    return (cosine, sine_table)


def rotate(key_heads, cosine, sine_table):
    half_dim = HEAD_DIM // 2
    turned = jnp.concatenate([-key_heads[..., half_dim:], key_heads[..., :half_dim]], axis=-1)
    return key_heads * cosine[:, None, :] + turned * sine_table[:, None, :]


def prepare(query_rows, kv_count, head_group):
    count_rows = query_rows.shape[0]
    shaped = query_rows.reshape(count_rows, kv_count, head_group, HEAD_DIM)
    return shaped.transpose(1, 2, 0, 3).reshape(kv_count, head_group * count_rows, HEAD_DIM)


def finish(summed, totals, count_rows, kv_count, head_group):
    blended = summed / totals[..., None]
    blended = blended.reshape(kv_count, head_group, count_rows, HEAD_DIM).transpose(2, 0, 1, 3)
    return blended.reshape(count_rows, kv_count * head_group * HEAD_DIM).astype(jnp.bfloat16)


def update(carry_state, query_set, positions, block_keys, block_values, key_start):
    running_max, running_sum, running_out = carry_state
    score_scale = 1.0 / math.sqrt(HEAD_DIM)
    scores = (
        jnp.einsum("grd,kgd->grk", query_set, block_keys, preferred_element_type=jnp.float32)
        * score_scale
    )
    key_pos = key_start + jnp.arange(block_keys.shape[0], dtype=jnp.int32)
    allowed = key_pos[None, None, :] <= positions[None, :, None]
    scores = jnp.where(allowed, scores, -1e30)
    new_max = jnp.maximum(running_max, jnp.max(scores, axis=-1))
    shrink = jnp.exp(running_max - new_max)
    weight = jnp.where(allowed, jnp.exp(scores - new_max[..., None]), 0.0)
    running_sum = running_sum * shrink + jnp.sum(weight, axis=-1)
    running_out = running_out * shrink[..., None] + jnp.einsum(
        "grk,kgd->grd",
        weight.astype(jnp.bfloat16),
        block_values,
        preferred_element_type=jnp.float32,
    )
    return (new_max, running_sum, running_out)


def body(queries, text_keys, text_values, image_features, kv_weight, image_grids):
    ctx_index = lax.axis_index("ctx")
    row_count = queries.shape[0]
    kv_width = text_keys.shape[1]
    kv_count = kv_width // HEAD_DIM
    head_group = queries.shape[1] // kv_width
    slot_count = GRID * GRID
    partial_kv = lax.dot_general(
        image_features, kv_weight, (((0,), (0,)), ((), ())), preferred_element_type=jnp.float32
    )
    feature_f32 = image_features.astype(jnp.float32)
    square_sums = jnp.sum(feature_f32 * feature_f32, axis=0)
    raw_kv, power_total = (
        lax.psum_scatter(partial_kv, "ctx", scatter_dimension=0, tiled=True),
        lax.psum_scatter(square_sums, "ctx", scatter_dimension=0, tiled=True),
    )
    normed = raw_kv * lax.rsqrt(power_total / D + 1e-06)[:, None]
    offset = image_grids[0, 0]
    grid_tall = image_grids[0, 1]
    grid_wide = image_grids[0, 2]
    within = jnp.arange(slot_count, dtype=jnp.int32)
    image_start = ctx_index * row_count + offset
    time_ids = jnp.broadcast_to(image_start, (slot_count,))
    height_ids = image_start + within // grid_wide
    width_ids = image_start + within % grid_wide
    cosine, sine_table = rope_tables(time_ids, height_ids, width_ids)
    key_heads = normed[:, :kv_width].reshape(slot_count, kv_count, HEAD_DIM)
    image_keys = (
        rotate(key_heads, cosine, sine_table).reshape(slot_count, kv_width).astype(jnp.bfloat16)
    )
    image_values = normed[:, kv_width:].astype(jnp.bfloat16)
    live_slot = within < grid_tall * grid_wide
    local_rows = jnp.arange(row_count, dtype=jnp.int32)
    one_hot = ((local_rows[:, None] == offset + within[None, :]) & live_slot[None, :]).astype(
        jnp.bfloat16
    )
    image_rows = (local_rows >= offset) & (local_rows < offset + grid_tall * grid_wide)
    placed = jnp.dot(
        one_hot,
        jnp.concatenate([image_keys, image_values], axis=1),
        preferred_element_type=jnp.float32,
    ).astype(jnp.bfloat16)
    cache_keys = jnp.where(image_rows[:, None], placed[:, :kv_width], text_keys)
    cache_values = jnp.where(image_rows[:, None], placed[:, kv_width:], text_values)
    half_rows = row_count // 2
    lead_queries = queries[:half_rows]
    trail_queries = queries[half_rows:]
    trail_base = ctx_index * row_count + half_rows
    lead_base = ctx_index * row_count
    query_sets = jnp.stack(
        [prepare(lead_queries, kv_count, head_group), prepare(trail_queries, kv_count, head_group)]
    )
    query_span = head_group * half_rows
    row_pos = jnp.arange(query_span, dtype=jnp.int32) % half_rows
    base_rows = jnp.stack([lead_base, trail_base])
    query_pos = base_rows[:, None] + row_pos[None, :]
    limits = base_rows + half_rows - 1
    initial = (
        jnp.full((2, kv_count, query_span), -1e30, jnp.float32),
        jnp.zeros((2, kv_count, query_span), jnp.float32),
        jnp.zeros((2, kv_count, query_span, HEAD_DIM), jnp.float32),
    )
    piece_keys = lax.all_gather(cache_keys, "ctx", axis=0, tiled=True)
    piece_values = lax.all_gather(cache_values, "ctx", axis=0, tiled=True)
    piece_size = piece_keys.shape[0]
    block_size = math.gcd(piece_size, 512)
    block_count = piece_size // block_size
    split_keys = piece_keys.reshape(block_count, block_size, kv_count, HEAD_DIM)
    split_values = piece_values.reshape(block_count, block_size, kv_count, HEAD_DIM)

    def scan_step(carried_state, scan_item):
        block_keys, block_values, number = scan_item
        key_start = number * block_size
        outcome = []
        for half_index in range(2):
            half_state = tuple((member[half_index] for member in carried_state))
            updated = lax.cond(
                key_start <= limits[half_index],
                lambda current: update(
                    current,
                    query_sets[half_index],
                    query_pos[half_index],
                    block_keys,
                    block_values,
                    key_start,
                ),
                lambda current: current,
                half_state,
            )
            outcome.append(updated)
        stacked = tuple(
            (
                jnp.stack([outcome[0][number_index], outcome[1][number_index]])
                for number_index in range(3)
            )
        )
        return (stacked, None)

    result_state, unused_out = lax.scan(
        scan_step, initial, (split_keys, split_values, jnp.arange(block_count, dtype=jnp.int32))
    )
    running_max, running_sum, running_out = result_state
    lead_out = finish(running_out[0], running_sum[0], half_rows, kv_count, head_group)
    trail_out = finish(running_out[1], running_sum[1], half_rows, kv_count, head_group)
    attention = jnp.concatenate([lead_out, trail_out], axis=0)
    return (attention, cache_keys, cache_values)


def solution(mesh):
    in_specs = (
        P(("groups", "ctx"), None),
        P(("groups", "ctx"), None),
        P(("groups", "ctx"), None),
        P(("groups", "ctx"), None),
        P("ctx", None),
        P(("groups", "ctx"), None),
    )
    out_specs = (P(("groups", "ctx"), None), P(("groups", "ctx"), None), P(("groups", "ctx"), None))
    return jax.shard_map(body, mesh=mesh, in_specs=in_specs, out_specs=out_specs, check_vma=False)
```

profile of v0, /device:TPU:25, one launch (start us, length us, event | category | flops | bytes accessed | tf_op | source)
XLA Modules:
  0.0 195.6 jit_solution(3191314341069254623)
XLA Ops:
  7.3 1.1 copy-done
  8.4 2.4 %fusion.47 = f32[256,1024]{1,0:T(8,128)} fusion(bf16[512,256]{1,0:T(8,128)(2,1)} %param.15, bf16[512,1024]{1,0:T(8,128)(2,1)S(1)} %copy-done), kind=kOutput, calls=%fused_computation.104 | convolution fusion | flops 268435456 | bytes 2359296 | tf_op jit(solution)/shard_map/dot_general | solution.py:78
  10.9 0.6 fusion.46
  16.1 0.6 dynamic-slice
  17.4 25.9 %all-reduce = f32[256]{0:T(256)S(1)} all-reduce(f32[256]{0:T(256)S(1)} %multiply_reduce_fusion), channel_id=3, replica_groups=mesh['groups'=2,'ctx'=16] {'ctx'}, use_global_device_ids=true, to_apply=%region_2.0.clone | all-reduce | flops 256 | bytes 2048
  43.3 0.7 iota_add_fusion.2
  44.0 0.7 compare_and_fusion
  44.7 0.8 fusion.39
  45.8 21.4 %reduce-scatter.2.cloned.1.call-done = f32[16,1024]{1,0:T(8,128)} async-done(((f32[256,1024]{1,0:T(8,128)}), f32[16,1024]{1,0:T(8,128)}) %reduce-scatter.2.cloned.1.call-update) | async-done | bytes 65552 | tf_op jit(solution)/shard_map/reduce_scatter | solution.py:84
  67.1 0.9 broadcast_multiply_fusion
  68.3 0.2 convolution_convert_fusion
  68.5 0.7 slice_select_fusion
  69.3 0.7 all-gather.5.cloned.1.call-update
  70.3 0.8 copy.26
  71.2 38.2 %all-gather.3.cloned.1.call-done = bf16[1024,512]{1,0:T(8,128)(2,1)} async-done(((bf16[64,512]{1,0:T(8,128)(2,1)}), bf16[1024,512]{1,0:T(8,128)(2,1)}) %all-gather.3.cloned.1.call-update) | async-done | bytes 1048592 | tf_op jit(solution)/shard_map/all_gather | solution.py:133
  109.4 2.2 %reshape.193 = bf16[2,512,4,128]{3,2,1,0:T(4,128)(2,1)} reshape(bf16[1024,512]{1,0:T(8,128)(2,1)} %all-gather.3.cloned.1.call-done) | data formatting | bytes 2097152 | tf_op jit(solution)/shard_map/reshape | solution.py:138
  111.5 37.7 %all-gather.5.cloned.1.call-done = bf16[1024,512]{1,0:T(8,128)(2,1)} async-done(((bf16[64,512]{1,0:T(8,128)(2,1)}), bf16[1024,512]{1,0:T(8,128)(2,1)}) %all-gather.5.cloned.1.call-update) | async-done | bytes 1048592 | tf_op jit(solution)/shard_map/all_gather | solution.py:134
  149.2 2.1 %reshape.194 = bf16[2,512,4,128]{3,2,1,0:T(4,128)(2,1)} reshape(bf16[1024,512]{1,0:T(8,128)(2,1)} %all-gather.5.cloned.1.call-done) | data formatting | bytes 2097152 | tf_op jit(solution)/shard_map/reshape | solution.py:139
  151.5 35.4 %while.15 = (s32[]{:T(128)}, f32[2,4,256]{2,1,0:T(4,128)S(1)}, f32[2,4,256]{2,1,0:T(4,128)S(1)}, f32[2,4,256,128]{3,2,1,0:T(8,128)S(1)}, s32[2]{0:T(128)S(1)}, /...) while((s32[]{:T(128)}, f32[2,4,256]{2,1,0:T(4,128)S(1)}, ...), condition=%wide.region_12.13_spmd.clone, body=%wide.region_3.12_spmd.clone.sunk | while | flops 551560704 | bytes 36390424 | solution.py:169
  151.5 0.7 dynamic_slice.19
  152.8 0.6 fusion.57
  154.1 0.6 slice_bitcast_fusion.10
  154.8 0.5 copy-done.1
  155.3 0.3 copy-done.2
  155.6 0.4 constant_dynamic-slice_fusion.3
  156.1 0.7 copy.87
  156.8 5.1 %conditional.6 = (f32[1,4,256]{2,1,0:T(4,128)}, f32[1,4,256]{2,1,0:T(4,128)S(1)}, f32[1,4,256,128]{3,2,1,0:T(8,128)S(1)}) conditional(s32[]{:T(128)} %convert_element_type.81, (f32[4,256]{1,0:T(4,128)}, f32[4,256]{1,0:T(4,128)S(1)}, f32[4,256,128]{2,1,0:T(8,128)S(1)}) %tuple.139, (s32[]{:T(128)}, s32[2,256]{1,0:T(2,128)S(1)}, ...), branch_computations={%region_8.8_spmd, %region_9.11_spmd} | conditional | flops 275646976 | bytes 9239580 | solution.py:147
  157.0 0.6 fusion.14
  157.6 0.6 max.5
  158.2 1.5 fusion.16
  159.7 0.7 add_bitcast_fusion.1
  160.4 1.6 fusion.17
  162.6 0.7 copy.93
  163.3 5.1 %conditional.7 = (f32[1,4,256]{2,1,0:T(4,128)}, f32[1,4,256]{2,1,0:T(4,128)S(1)}, f32[1,4,256,128]{3,2,1,0:T(8,128)S(1)}) conditional(s32[]{:T(128)} %convert_element_type.82, (f32[4,256]{1,0:T(4,128)}, f32[4,256]{1,0:T(4,128)S(1)}, f32[4,256,128]{2,1,0:T(8,128)S(1)}) %tuple.141, (s32[]{:T(128)}, s32[2,256]{1,0:T(2,128)S(1)}, ...), branch_computations={%region_4.4_spmd, %region_5.7_spmd} | conditional | flops 275646976 | bytes 9239580 | solution.py:147
  163.4 0.6 fusion.2
  164.0 0.6 max.4
  164.6 1.5 fusion.4
  166.1 0.7 add_bitcast_fusion
  166.8 1.6 fusion.5
  168.4 0.7 pad_maximum_fusion.9
  169.2 0.7 dynamic_slice.19
  170.5 0.6 fusion.57
  171.8 0.6 slice_bitcast_fusion.10
  172.5 0.5 copy-done.1
  173.0 0.3 copy-done.2
  173.3 0.4 constant_dynamic-slice_fusion.3
  173.8 0.7 copy.87
  174.5 5.1 %conditional.6 = (f32[1,4,256]{2,1,0:T(4,128)}, f32[1,4,256]{2,1,0:T(4,128)S(1)}, f32[1,4,256,128]{3,2,1,0:T(8,128)S(1)}) conditional(s32[]{:T(128)} %convert_element_type.81, (f32[4,256]{1,0:T(4,128)}, f32[4,256]{1,0:T(4,128)S(1)}, f32[4,256,128]{2,1,0:T(8,128)S(1)}) %tuple.139, (s32[]{:T(128)}, s32[2,256]{1,0:T(2,128)S(1)}, ...), branch_computations={%region_8.8_spmd, %region_9.11_spmd} | conditional | flops 275646976 | bytes 9239580 | solution.py:147
  174.7 0.6 fusion.14
  175.3 0.6 max.5
  175.9 1.5 fusion.16
  177.4 0.7 add_bitcast_fusion.1
  178.1 1.6 fusion.17
  180.3 0.7 copy.93
  181.0 5.1 %conditional.7 = (f32[1,4,256]{2,1,0:T(4,128)}, f32[1,4,256]{2,1,0:T(4,128)S(1)}, f32[1,4,256,128]{3,2,1,0:T(8,128)S(1)}) conditional(s32[]{:T(128)} %convert_element_type.82, (f32[4,256]{1,0:T(4,128)}, f32[4,256]{1,0:T(4,128)S(1)}, f32[4,256,128]{2,1,0:T(8,128)S(1)}) %tuple.141, (s32[]{:T(128)}, s32[2,256]{1,0:T(2,128)S(1)}, ...), branch_computations={%region_4.4_spmd, %region_5.7_spmd} | conditional | flops 275646976 | bytes 9239580 | solution.py:147
  181.1 0.6 fusion.2
  181.7 0.6 max.4
  182.3 1.5 fusion.4
  183.8 0.7 add_bitcast_fusion
  184.5 1.6 fusion.5
  186.1 0.7 pad_maximum_fusion.9
  187.1 0.4 fusion.26
  187.8 0.4 fusion.27
  188.3 0.8 pad_maximum_fusion.3
  (83 shorter events, 3.2 us)
Async XLA Ops:
  7.2 1.2 copy-start
  7.2 8.9 %copy-start.9 = (u32[32]{0:T(128)S(1)}, u32[32]{0:T(128)}, u32[]{:S(2)}) copy-start(u32[32]{0:T(128)} %constant.92) | copy-start | bytes 388
  7.2 10.1 %copy-start.4 = (bf16[512,256]{1,0:T(8,128)(2,1)S(1)}, bf16[512,256]{1,0:T(8,128)(2,1)}, u32[]{:S(2)}) copy-start(bf16[512,256]{1,0:T(8,128)(2,1)} %param.15) | copy-start | bytes 786436
  7.2 3.7 %copy-start.8 = (s32[1,3]{1,0:T(1,128)S(1)}, s32[1,3]{1,0:T(1,128)}, u32[]{:S(2)}) copy-start(s32[1,3]{1,0:T(1,128)} %param.17) | copy-start | bytes 40
  7.2 61.3 %copy-start.6 = (bf16[64,512]{1,0:T(8,128)(2,1)S(1)}, bf16[64,512]{1,0:T(8,128)(2,1)}, u32[]{:S(2)}) copy-start(bf16[64,512]{1,0:T(8,128)(2,1)} %param.14) | copy-start | bytes 196612
  7.2 61.3 %copy-start.7 = (bf16[64,512]{1,0:T(8,128)(2,1)S(1)}, bf16[64,512]{1,0:T(8,128)(2,1)}, u32[]{:S(2)}) copy-start(bf16[64,512]{1,0:T(8,128)(2,1)} %param.13) | copy-start | bytes 196612
  7.2 62.8 %copy-start.5 = (bf16[64,4096]{1,0:T(8,128)(2,1)S(1)}, bf16[64,4096]{1,0:T(8,128)(2,1)}, u32[]{:S(2)}) copy-start(bf16[64,4096]{1,0:T(8,128)(2,1)} %param.12) | copy-start | bytes 1572868
  7.2 59.9 %reduce-scatter.2.cloned.1.call-start = ((), (), s32[]{:S(2)}) async-start(), calls=%async_computation.1 | async-start | bytes 1114112 | tf_op jit(solution)/shard_map/reduce_scatter | solution.py:84
  10.8 98.5 %all-gather.3.cloned.1.call-start = ((), (), s32[]{:S(2)}) async-start(), calls=%async_computation.2 | async-start | bytes 1114112 | tf_op jit(solution)/shard_map/all_gather | solution.py:133
  69.3 80.0 %all-gather.5.cloned.1.call-start = ((), (), s32[]{:S(2)}) async-start(), calls=%async_computation.3 | async-start | bytes 1114112 | tf_op jit(solution)/shard_map/all_gather | solution.py:134
  154.1 1.2 copy-start.1
  154.1 1.5 copy-start.2
  155.6 1.2 copy-start.3
  171.8 1.2 copy-start.1
  171.8 1.5 copy-start.2
  173.3 1.2 copy-start.3
Sparse Core Ops, SparseCore 0:
  11.7 55.4 reduce-scatter.1
  70.1 39.2 all-gather.2
  112.4 36.8 all-gather.4
where the time goes:
time: 197 us; the launch traced here: 196 us
  waiting for transfers between devices  98 us (50%)
  blocking collectives  25.9 us (13%)
  other arithmetic  19.3 us (10%)
  between operations  19.2 us (10%)
  local copies, waits for them, and re-layouts  17.6 us (9%)
  matrix products  11.3 us (6%)
  loops' own time  4.18 us (2%)
    all_gather x1, waiting for transfers between devices, body(): piece_keys = lax.all_gather(cache_keys, 'ctx', axis=0, tiled=True)  38.2 us
    all_gather x1, waiting for transfers between devices, body(): piece_values = lax.all_gather(cache_values, 'ctx', axis=0, tiled=True)  37.7 us
    unnamed x1, blocking collectives  25.9 us
    reduce_scatter x1, waiting for transfers between devices, body(): lax.psum_scatter(partial_kv, 'ctx', scatter_dimension=0, tiled=True)  21.4 us
    dot_general x4, matrix products, update(): jnp.einsum('grk,kgd->grd', weight.astype(jnp.bfloat16), block_values, pre...  6.44 us
    reduce_sum x4, other arithmetic, update(): running_sum = running_sum * shrink + jnp.sum(weight, axis=-1)  5.93 us
    while x16, local copies, waits for them, and re-layouts  4.29 us
    another operation x10, other arithmetic, scan_step(): jnp.stack([outcome[0][number_index], outcome[1][number_index]])  4.27 us
  transfers between devices with their start and end apart: 3, of which 3 were waited for; matrix products, arithmetic and copies ran while one was open for 4% of the time, Pallas kernels for 0%

commit v1 on v0

v1 whole, which is shorter than its diff:
```python
import functools
import math

import jax
import jax.numpy as jnp
import numpy as np
from jax import lax
from jax.experimental import pallas as pl
from jax.experimental.pallas import tpu as pltpu
from jax.sharding import PartitionSpec as P

HEAD_DIM = 128
GRID = 4
SLOTS = GRID * GRID
BIG = 1 << 30
NEG = -1e30
F32 = jnp.float32
BF16 = jnp.bfloat16


def dot(x, y, cx, cy):
    return lax.dot_general(x, y, (((cx,), (cy,)), ((), ())), preferred_element_type=F32)


def kernel(
    n, inner,
    q_ref, tk_ref, tv_ref, feat_ref, w_ref, grid_ref, freq_ref,
    out_ref, ck_ref, cv_ref,
    tkv, img, meta, mine, p1_src, p1_dst, p2_src, p2_dst, qs, pos_t, pos_i, m_ref, acc_ref,
    meta_s, meta_r, p1_s, p1_r, p2_s, p2_r,
    tz_s, ty_s, t_r, tm_s, tm_r, i_s, i_r, im_s, im_r,
):
    chips = n // 2
    outer = chips // inner
    rows, width = tk_ref.shape
    kv = width // HEAD_DIM
    group = q_ref.shape[1] // width
    feats, slots = feat_ref.shape
    pair = 2 * SLOTS
    total_features = feats * n
    me = lax.axis_index("ctx")
    core = lax.rem(me, 2)
    chip = me // 2
    a = chip // inner
    b = lax.rem(chip, inner)
    mate = me + 1 - 2 * core

    def loop(low, high, f):
        lax.fori_loop(low, high, lambda i, c: (f(i), c)[1], 0)

    def copy(src, dst, send, recv, target):
        return pltpu.make_async_remote_copy(
            src_ref=src, dst_ref=dst, send_sem=send, recv_sem=recv,
            device_id={"ctx": target}, device_id_type=pl.DeviceIdType.MESH,
        )

    own = pl.ds(pl.multiple_of(me * rows, rows), rows)
    tkv[own, :width] = tk_ref[...]
    tkv[own, width:] = tv_ref[...]
    offset, tall, wide = grid_ref[0, 0], grid_ref[0, 1], grid_ref[0, 2]
    line = lax.broadcasted_iota(jnp.int32, (8, 128), 0)
    meta[me] = jnp.where(line == 0, offset, jnp.where(line == 1, tall, wide))
    img[...] = jnp.zeros_like(img)

    barrier = pltpu.get_barrier_semaphore()
    loop(1, n, lambda d: pl.semaphore_signal(
        barrier, inc=1, device_id={"ctx": lax.rem(me + d, n)},
        device_id_type=pl.DeviceIdType.MESH))
    pl.semaphore_wait(barrier, n - 1)

    def block(j):
        shard = 2 * j + core
        return tkv.at[pl.ds(pl.multiple_of(shard * rows, rows), rows), :]

    def meta_copy(d):
        return copy(meta.at[me], meta.at[me], meta_s.at[d], meta_r.at[me], lax.rem(me + d, n))

    def meta_in(j):
        return copy(meta.at[j], meta.at[j], meta_s.at[0], meta_r.at[j], mate)

    def up_copy(to):
        return copy(block(chip), block(chip), tz_s.at[to], t_r.at[chip],
                    2 * (to * inner + b) + core)

    def side_copy(from_a, d):
        j = from_a * inner + b
        return copy(block(j), block(j), ty_s.at[from_a * inner + d], t_r.at[j],
                    2 * (a * inner + lax.rem(b + d, inner)) + core)

    def t_in(j):
        return copy(block(j), block(j), tz_s.at[0], t_r.at[j], mate)

    def t_mate(j):
        return copy(block(j), block(j), tm_s.at[j], tm_r.at[j], mate)

    def t_mate_in(j):
        shard = 2 * j + 1 - core
        ref = tkv.at[pl.ds(pl.multiple_of(shard * rows, rows), rows), :]
        return copy(ref, ref, tm_s.at[j], tm_r.at[j], mate)

    loop(1, n, lambda d: meta_copy(d).start())

    half = lambda c: w_ref[:, pl.ds(pl.multiple_of(c * width, width), width)]
    features = feat_ref[...]
    p1_src[:, :width] = dot(features, half(1 - core), 0, 0).astype(BF16)
    wide_f = features.astype(F32)
    square = wide_f * wide_f
    high = square.astype(BF16)
    low = (square - high.astype(F32)).astype(BF16)
    ones = jnp.ones((feats, 128), BF16)
    power = dot(high, ones, 0, 0) + dot(low, ones, 0, 0)
    lane_s = lax.broadcasted_iota(jnp.int32, (slots, 128), 1)

    def split(x):
        top = x.astype(BF16)
        return jnp.where(lane_s < 64, top, (x - top.astype(F32)).astype(BF16))

    p1_src[:, width:] = split(power)
    p1 = copy(p1_src, p1_dst, p1_s, p1_r, mate)
    p1.start()
    mine[:, :width] = dot(features, half(core), 0, 0)
    mine[:, width:] = power
    p1.wait_recv()
    mine[:, :width] = mine[:, :width] + p1_dst[:, :width].astype(F32)
    other = p1_dst[:, width:].astype(F32)
    power = power + other[:, 0:1] + other[:, 64:65]
    mine[:, width:] = power
    p2_src[:, :width] = mine[:, :width].astype(BF16)
    p2_src[:, width:] = split(power)

    def p2_copy(d):
        j = lax.rem(chip + d, chips)
        return copy(p2_src.at[pl.ds(pl.multiple_of(j * pair, pair), pair), :], p2_dst.at[chip],
                    p2_s.at[d], p2_r.at[chip], 2 * j + core)

    def p2_in(j):
        return copy(p2_dst.at[j], p2_dst.at[j], p2_s.at[0], p2_r.at[j], mate)

    loop(1, chips, lambda d: p2_copy(d).start())
    loop(a + 1, outer, lambda to: up_copy(to).start())
    loop(1, inner, lambda d: side_copy(a, d).start())
    t_mate(chip).start()

    for g in range(kv):
        for h in range(group):
            at = (g * group + h) * HEAD_DIM
            qs[g, h * rows:(h + 1) * rows, :] = q_ref[:, at:at + HEAD_DIM]

    def meta_wait(d):
        meta_in(lax.rem(me + d, n)).wait_recv()

    loop(1, n, meta_wait)
    lane_t = lax.broadcasted_iota(jnp.int32, pos_t.shape, 1)
    lane_i = lax.broadcasted_iota(jnp.int32, pos_i.shape, 1)

    def place(j, carry):
        text, image = carry
        o, t, w = meta[j, 0:1, 0:1], meta[j, 1:2, 0:1], meta[j, 2:3, 0:1]
        begin = j * rows + o
        dead = (lane_t >= begin) & (lane_t < begin + t * w)
        k = lane_i - j * SLOTS
        live = (k >= 0) & (k < t * w)
        return jnp.where(dead, BIG, text), jnp.where(live, begin + k, image)

    text, image = lax.fori_loop(0, n, place, (lane_t, jnp.full(pos_i.shape, BIG, jnp.int32)))
    pos_t[...] = text
    pos_i[...] = image

    row = lax.broadcasted_iota(jnp.int32, (pair, 128), 0)
    lane = lax.broadcasted_iota(jnp.int32, (pair, 128), 1)
    second = row >= SLOTS
    k = jnp.where(second, row - SLOTS, row)
    pick = lambda i: jnp.where(second, meta[2 * chip + 1, i:i + 1, :], meta[2 * chip, i:i + 1, :])
    gw = pick(2)
    gy = jnp.zeros_like(k)
    for i in range(1, SLOTS // 2):
        gy = gy + jnp.where(k >= i * gw, 1, 0)
    gx = k - gy * gw
    t_id = (2 * chip + jnp.where(second, 1, 0)) * rows + pick(0)
    j = jnp.where(lane >= HEAD_DIM // 2, lane - HEAD_DIM // 2, lane)
    first_bound = HEAD_DIM // 8
    second_bound = first_bound + 3 * HEAD_DIM // 16
    ids = t_id + jnp.where(j < first_bound, 0, jnp.where(j < second_bound, gy, gx))
    angle = ids.astype(F32) * freq_ref[...]
    is_key = core == 0
    cosine = jnp.where(is_key, jnp.cos(angle), 1.0)
    sine = jnp.where(is_key, jnp.sin(angle), 0.0)
    sine = jnp.where(lane < HEAD_DIM // 2, -sine, sine)

    mine_rows = pl.ds(pl.multiple_of(chip * pair, pair), pair)

    def add(d, carry):
        total, extra = carry
        src = lax.rem(chip + d, chips)
        p2_in(src).wait_recv()
        return (total + p2_dst[src, :, :width].astype(F32),
                extra + p2_dst[src, :, width:].astype(F32))

    total, extra = lax.fori_loop(
        1, chips, add, (mine[mine_rows, :width], jnp.zeros((pair, 128), F32)))
    power = mine[mine_rows, width:] + extra[:, 0:1] + extra[:, 64:65]
    scale = lax.rsqrt(power / total_features + 1e-6)
    for h in range(kv):
        at = slice(h * HEAD_DIM, (h + 1) * HEAD_DIM)
        x = total[:, at] * scale
        turned = jnp.concatenate([x[:, HEAD_DIM // 2:], x[:, :HEAD_DIM // 2]], axis=1)
        img[core, chip, :, at] = (x * cosine + turned * sine).astype(BF16)

    def i_copy(j):
        return copy(img.at[core, chip], img.at[core, chip], i_s.at[j], i_r.at[chip], 2 * j + core)

    def i_in(j):
        return copy(img.at[core, j], img.at[core, j], i_s.at[0], i_r.at[j], mate)

    def i_mate(j):
        return copy(img.at[core, j], img.at[core, j], im_s.at[j], im_r.at[j], mate)

    def i_mate_in(j):
        return copy(img.at[1 - core, j], img.at[1 - core, j], im_s.at[j], im_r.at[j], mate)

    def others(low, high, f):
        def step(j):
            @pl.when(j != chip)
            def _():
                f(j)
        loop(low, high, step)

    seen = (a + 1) * inner
    others(a * inner, chips, lambda j: i_copy(j).start())
    i_mate(chip).start()

    def pass_on(i):
        from_a = a - 1 - i
        j = from_a * inner + b
        t_in(j).wait_recv()
        loop(1, inner, lambda d: side_copy(from_a, d).start())
        t_mate(j).start()

    loop(0, a, pass_on)

    def from_side(i):
        from_a = a - i

        def step(d):
            j = from_a * inner + lax.rem(b + d, inner)
            t_in(j).wait_recv()
            t_mate(j).start()

        loop(1, inner, step)

    loop(0, a + 1, from_side)

    def image_on(j):
        i_in(j).wait_recv()
        i_mate(j).start()

    others(0, seen, image_on)
    loop(0, seen, lambda j: t_mate_in(j).wait_recv())

    span = group * rows
    plane = 2 * inner * rows
    q_pos = me * rows + lax.rem(lax.broadcasted_iota(jnp.int32, (span, 1), 0), rows)
    factor = math.log2(math.e) / math.sqrt(HEAD_DIM)

    def attend(g, keys, values, pos):
        s = dot(qs[g], keys, 1, 1)
        s = jnp.where(pos <= q_pos, s, NEG)
        before = m_ref[g]
        now = jnp.maximum(before, jnp.max(s, axis=1, keepdims=True))
        shrink = jnp.exp2((before - now) * factor)
        weight = jnp.exp2((s - now[:, 0:1]) * factor).astype(BF16)
        both = jnp.concatenate([values, jnp.ones_like(values)], axis=1)
        product = dot(weight, both, 1, 0)
        acc_ref[g, :, :HEAD_DIM] = acc_ref[g, :, :HEAD_DIM] * shrink + product[:, :HEAD_DIM]
        acc_ref[g, :, HEAD_DIM:] = acc_ref[g, :, HEAD_DIM:] * shrink + product[:, HEAD_DIM:]
        m_ref[g] = now

    m_ref[...] = jnp.full(m_ref.shape, NEG, F32)
    acc_ref[...] = jnp.zeros_like(acc_ref)

    def text_step(p):
        at = pl.ds(pl.multiple_of(p * plane, plane), plane)
        pos = pos_t[:, at]
        for g in range(kv):
            lo = g * HEAD_DIM
            attend(g, tkv[at, lo:lo + HEAD_DIM], tkv[at, width + lo:width + lo + HEAD_DIM], pos)

    loop(0, a + 1, text_step)

    loop(0, seen, lambda j: i_mate_in(j).wait_recv())
    local = lax.broadcasted_iota(jnp.int32, (rows, SLOTS), 0)
    within = lax.broadcasted_iota(jnp.int32, (rows, SLOTS), 1)
    count = tall * wide
    hot = jnp.where((local == offset + within) & (within < count), 1.0, 0.0).astype(BF16)
    local = lax.broadcasted_iota(jnp.int32, (rows, width), 0)
    is_image = (local >= offset) & (local < offset + count)
    mine_slots = pl.ds(pl.multiple_of(core * SLOTS, SLOTS), SLOTS)
    for part, (ref, text_ref) in enumerate(((ck_ref, tk_ref), (cv_ref, tv_ref))):
        placed = dot(hot, img[part, chip, mine_slots, :], 1, 0)
        ref[...] = jnp.where(is_image, placed, text_ref[...].astype(F32)).astype(BF16)
    for g in range(kv):
        at = slice(g * HEAD_DIM, (g + 1) * HEAD_DIM)
        keys = img[0, :, :, at].reshape(slots, HEAD_DIM)
        values = img[1, :, :, at].reshape(slots, HEAD_DIM)
        attend(g, keys, values, pos_i[...])
        done = acc_ref[g, :, :HEAD_DIM] / acc_ref[g, :, HEAD_DIM:]
        for h in range(group):
            at = (g * group + h) * HEAD_DIM
            out_ref[:, at:at + HEAD_DIM] = done[h * rows:(h + 1) * rows].astype(BF16)

    loop(1, n, lambda d: meta_copy(d).wait_send())
    p1.wait_send()
    loop(1, chips, lambda d: p2_copy(d).wait_send())
    loop(a + 1, outer, lambda to: up_copy(to).wait_send())
    loop(0, a + 1, lambda f: loop(1, inner, lambda d: side_copy(f, d).wait_send()))
    loop(0, seen, lambda j: t_mate(j).wait_send())
    others(a * inner, chips, lambda j: i_copy(j).wait_send())
    loop(0, seen, lambda j: i_mate(j).wait_send())


def body(n, queries, text_keys, text_values, image_features, kv_weight, image_grids):
    chips = n // 2
    inner = 1
    while (2 * inner) ** 2 <= chips and chips % (2 * inner) == 0:
        inner *= 2
    outer = chips // inner
    rows, width = text_keys.shape
    kv = width // HEAD_DIM
    span = queries.shape[1] // width * rows
    slots = image_features.shape[1]
    pair = 2 * SLOTS
    j = np.arange(HEAD_DIM, dtype=np.float64) % (HEAD_DIM // 2)
    freq = jnp.asarray((1000000.0 ** (-2.0 * j / HEAD_DIM)).astype(np.float32)[None, :])
    dma = pltpu.SemaphoreType.DMA
    vmem = pl.BlockSpec(memory_space=pltpu.VMEM)
    smem = pl.BlockSpec(memory_space=pltpu.SMEM)
    return pl.pallas_call(
        functools.partial(kernel, n, inner),
        out_shape=(
            jax.ShapeDtypeStruct(queries.shape, BF16),
            jax.ShapeDtypeStruct(text_keys.shape, BF16),
            jax.ShapeDtypeStruct(text_values.shape, BF16),
        ),
        in_specs=[vmem] * 5 + [smem, vmem],
        out_specs=(vmem,) * 3,
        scratch_shapes=[
            pltpu.VMEM((n * rows, 2 * width), BF16),
            pltpu.VMEM((2, chips, pair, width), BF16),
            pltpu.VMEM((n, 8, 128), jnp.int32),
            pltpu.VMEM((slots, width + 128), F32),
            pltpu.VMEM((slots, width + 128), BF16),
            pltpu.VMEM((slots, width + 128), BF16),
            pltpu.VMEM((slots, width + 128), BF16),
            pltpu.VMEM((chips, pair, width + 128), BF16),
            pltpu.VMEM((kv, span, HEAD_DIM), BF16),
            pltpu.VMEM((1, n * rows), jnp.int32),
            pltpu.VMEM((1, slots), jnp.int32),
            pltpu.VMEM((kv, span, HEAD_DIM), F32),
            pltpu.VMEM((kv, span, 2 * HEAD_DIM), F32),
            dma((n,)), dma((n,)), dma, dma, dma((chips,)), dma((chips,)),
            dma((outer,)), dma((chips,)), dma((chips,)), dma((chips,)), dma((chips,)),
            dma((chips,)), dma((chips,)), dma((chips,)), dma((chips,)),
        ],
        compiler_params=pltpu.CompilerParams(
            collective_id=0, has_side_effects=True, vmem_limit_bytes=60 * 1024 * 1024
        ),
        cost_estimate=pl.CostEstimate(
            flops=4 * n * rows * queries.size, bytes_accessed=4 * queries.size,
            transcendentals=n * rows * rows * 32),
    )(queries, text_keys, text_values, image_features, kv_weight, image_grids, freq)


def solution(mesh):
    both = P(("groups", "ctx"), None)
    return jax.shard_map(
        functools.partial(body, mesh.shape["ctx"]), mesh=mesh,
        in_specs=(both, both, both, both, P("ctx", None), both),
        out_specs=(both, both, both), check_vma=False)
```

time: 197 us -> 56.9 us (0.29)
  waiting for transfers between devices: 98 us -> 0 us
  Pallas kernels: 0 us -> 52.7 us
  blocking collectives: 25.9 us -> 0 us
  other arithmetic: 19.3 us -> 0 us
  between operations: 19.2 us -> 0.65 us
  local copies, waits for them, and re-layouts: 17.6 us -> 3.4 us
  matrix products: 11.3 us -> 0 us
  loops' own time: 4.18 us -> 0 us
    all_gather x2 -> x0, waiting for transfers between devices: 75.9 us -> none  [the longest x1 38.2 us: body(): piece_keys = lax.all_gather(cache_keys, 'ctx', axis=0, tiled=True)]
    pallas_call x0 -> x1, Pallas kernels: none -> 52.7 us  [body(): pl.pallas_call(functools.partial(kernel, n, inner), out_shape=(jax.ShapeD...]
    unnamed x1 -> x0, blocking collectives: 25.9 us -> none
    reduce_scatter x1 -> x0, waiting for transfers between devices: 21.4 us -> none  [body(): lax.psum_scatter(partial_kv, 'ctx', scatter_dimension=0, tiled=True)]
    dot_general x10 -> x0, matrix products: 11.3 us -> none  [the longest x4 6.44 us: update(): jnp.einsum('grk,kgd->grd', weight.astype(jnp.bfloat16), block_values, pre...]
    reduce_sum x5 -> x0, other arithmetic: 6.02 us -> none  [the longest x4 5.93 us: update(): running_sum = running_sum * shrink + jnp.sum(weight, axis=-1)]
    reshape x3 -> x0, local copies, waits for them, and re-layouts: 4.31 us -> none  [the longest x1 2.16 us: body(): split_keys = piece_keys.reshape(block_count, block_size, kv_count, HEAD_DIM)]
    while x16 -> x0, local copies, waits for them, and re-layouts: 4.29 us -> none
  transfers between devices with their start and end apart: 3 -> 0, of which waited for: 3 -> 0; matrix products, arithmetic and copies ran while one was open for 4% -> 0% of each run, Pallas kernels for 0% -> 0%
where the time goes in v1:
time: 56.9 us; the launch traced here: 56.7 us
  Pallas kernels  52.7 us (93%)
  local copies, waits for them, and re-layouts  3.4 us (6%)
  between operations  0.65 us (1%)
    pallas_call x1, Pallas kernels, body(): pl.pallas_call(functools.partial(kernel, n, inner), out_shape=(jax.ShapeD...  52.7 us
    unnamed x7, local copies, waits for them, and re-layouts  3.4 us

profile of v1, /device:TPU:25, one launch (start us, length us, event | category | flops | bytes accessed | tf_op | source)
XLA Modules:
  0.0 56.7 jit_solution(5266051772489071193)
XLA Ops:
  0.6 52.7 %shard_map.94 = (bf16[64,4096]{1,0:T(8,128)(2,1)}, bf16[64,512]{1,0:T(8,128)(2,1)}, bf16[64,512]{1,0:T(8,128)(2,1)}) custom-call(bf16[64,4096]{1,0:T(8,128)(2,1)} %q_ref.1, bf16[64,512]{1,0:T(8,128)(2,1)} %tk_ref.1, bf16[64,512]{1,0:T(8,128)(2,1)} %tv_ref.1, bf16[512,256]{1,0:T(8,128)(2,1)} %feat_ref.1, bf16[512,1024]{1,0:T(8,128)(2,1)} %w_ref.1, ...), custom_call_target="tpu_custom_call" | custom-call | flops 1073741824 | bytes 1048576 | tf_op jit(solution)/shard_map/pallas_call | solution.py:337
  53.3 0.0 copy-start.1
  53.3 1.9 %copy.13 = bf16[64,4096]{1,0:T(8,128)(2,1)} copy(bf16[64,4096]{1,0:T(8,128)(2,1)} %get-tuple-element.6) | data formatting | bytes 1048576
  55.2 0.0 copy-done.1
  55.2 0.0 copy-start
  55.2 0.6 %copy.14 = bf16[64,512]{1,0:T(8,128)(2,1)} copy(bf16[64,512]{1,0:T(8,128)(2,1)S(1)} %copy-done.1) | data formatting | bytes 131072
  55.9 0.2 copy-done
  56.1 0.6 %copy.15 = bf16[64,512]{1,0:T(8,128)(2,1)} copy(bf16[64,512]{1,0:T(8,128)(2,1)S(1)} %copy-done) | data formatting | bytes 131072
Async XLA Ops:
  53.3 1.9 %copy-start.1 = (bf16[64,512]{1,0:T(8,128)(2,1)S(1)}, bf16[64,512]{1,0:T(8,128)(2,1)}, u32[]{:S(2)}) copy-start(bf16[64,512]{1,0:T(8,128)(2,1)} %get-tuple-element.7) | copy-start | bytes 196612
  55.2 0.9 %copy-start = (bf16[64,512]{1,0:T(8,128)(2,1)S(1)}, bf16[64,512]{1,0:T(8,128)(2,1)}, u32[]{:S(2)}) copy-start(bf16[64,512]{1,0:T(8,128)(2,1)} %get-tuple-element.8) | copy-start | bytes 196612

commit v2 on v1

--- a/solution.py
+++ b/solution.py
@@ -55,6 +55,7 @@
         )
 
     own = pl.ds(pl.multiple_of(me * rows, rows), rows)
+    tkv[:, width:] = jnp.zeros((n * rows, width), BF16)
     tkv[own, :width] = tk_ref[...]
     tkv[own, width:] = tv_ref[...]
     offset, tall, wide = grid_ref[0, 0], grid_ref[0, 1], grid_ref[0, 2]
@@ -99,16 +100,15 @@
         return copy(ref, ref, tm_s.at[j], tm_r.at[j], mate)
 
     loop(1, n, lambda d: meta_copy(d).start())
+    loop(a + 1, outer, lambda to: up_copy(to).start())
+    loop(1, inner, lambda d: side_copy(a, d).start())
 
     half = lambda c: w_ref[:, pl.ds(pl.multiple_of(c * width, width), width)]
-    features = feat_ref[...]
-    p1_src[:, :width] = dot(features, half(1 - core), 0, 0).astype(BF16)
+    features = feat_ref[...].T
+    p1_src[:, :width] = dot(features, half(1 - core), 1, 0).astype(BF16)
     wide_f = features.astype(F32)
-    square = wide_f * wide_f
-    high = square.astype(BF16)
-    low = (square - high.astype(F32)).astype(BF16)
-    ones = jnp.ones((feats, 128), BF16)
-    power = dot(high, ones, 0, 0) + dot(low, ones, 0, 0)
+    power = jnp.sum(wide_f * wide_f, axis=1, keepdims=True)
+    power = jnp.broadcast_to(power, (slots, 128))
     lane_s = lax.broadcasted_iota(jnp.int32, (slots, 128), 1)
 
     def split(x):
@@ -118,7 +118,7 @@
     p1_src[:, width:] = split(power)
     p1 = copy(p1_src, p1_dst, p1_s, p1_r, mate)
     p1.start()
-    mine[:, :width] = dot(features, half(core), 0, 0)
+    mine[:, :width] = dot(features, half(core), 1, 0)
     mine[:, width:] = power
     p1.wait_recv()
     mine[:, :width] = mine[:, :width] + p1_dst[:, :width].astype(F32)
@@ -137,8 +137,6 @@
         return copy(p2_dst.at[j], p2_dst.at[j], p2_s.at[0], p2_r.at[j], mate)
 
     loop(1, chips, lambda d: p2_copy(d).start())
-    loop(a + 1, outer, lambda to: up_copy(to).start())
-    loop(1, inner, lambda d: side_copy(a, d).start())
     t_mate(chip).start()
 
     for g in range(kv):
@@ -187,6 +185,15 @@
     sine = jnp.where(is_key, jnp.sin(angle), 0.0)
     sine = jnp.where(lane < HEAD_DIM // 2, -sine, sine)
 
+    def pass_on(i):
+        from_a = a - 1 - i
+        j = from_a * inner + b
+        t_in(j).wait_recv()
+        loop(1, inner, lambda d: side_copy(from_a, d).start())
+        t_mate(j).start()
+
+    loop(0, a, pass_on)
+
     mine_rows = pl.ds(pl.multiple_of(chip * pair, pair), pair)
 
     def add(d, carry):
@@ -229,15 +236,6 @@
     others(a * inner, chips, lambda j: i_copy(j).start())
     i_mate(chip).start()
 
-    def pass_on(i):
-        from_a = a - 1 - i
-        j = from_a * inner + b
-        t_in(j).wait_recv()
-        loop(1, inner, lambda d: side_copy(from_a, d).start())
-        t_mate(j).start()
-
-    loop(0, a, pass_on)
-
     def from_side(i):
         from_a = a - i
 
@@ -250,42 +248,63 @@
 
     loop(0, a + 1, from_side)
 
+    loop(0, seen, lambda j: t_mate_in(j).wait_recv())
+
+    span = group * rows
+    part = math.gcd(span, 256)
+    block_keys = math.gcd(n * rows, 1024)
+    key_blocks = n * rows // block_keys
+    factor = math.log2(math.e) / math.sqrt(HEAD_DIM)
+    q_pos = me * rows + lax.rem(lax.broadcasted_iota(jnp.int32, (part, 1), 0), rows)
+
+    def attend(g, r, keys, values, pos, first):
+        at = slice(r * part, (r + 1) * part)
+        s = dot(qs[g, at, :], keys, 1, 1)
+        s = jnp.where(pos <= q_pos, s, NEG)
+        now = jnp.broadcast_to(jnp.max(s, axis=1, keepdims=True), (part, HEAD_DIM))
+        if not first:
+            before = m_ref[g, at, :]
+            now = jnp.maximum(before, now)
+        shift = jnp.concatenate([now] * (s.shape[1] // HEAD_DIM), axis=1)
+        weight = jnp.exp2((s - shift) * factor).astype(BF16)
+        both = jnp.concatenate([values, jnp.ones_like(values)], axis=1)
+        product = dot(weight, both, 1, 0)
+        summed, totals = product[:, :HEAD_DIM], product[:, HEAD_DIM:]
+        if not first:
+            shrink = jnp.exp2((before - now) * factor)
+            summed = summed + acc_ref[g, at, :HEAD_DIM] * shrink
+            totals = totals + acc_ref[g, at, HEAD_DIM:] * shrink
+        return now, summed, totals
+
+    def text_block(g, r, p, first):
+        at = pl.ds(pl.multiple_of(p * block_keys, block_keys), block_keys)
+        lo = g * HEAD_DIM
+        now, summed, totals = attend(
+            g, r, tkv[at, lo:lo + HEAD_DIM], tkv[at, width + lo:width + lo + HEAD_DIM],
+            pos_t[:, at], first)
+        at = slice(r * part, (r + 1) * part)
+        m_ref[g, at, :] = now
+        acc_ref[g, at, :HEAD_DIM] = summed
+        acc_ref[g, at, HEAD_DIM:] = totals
+
+    def text_heads(heads):
+        for g in heads:
+            for r in range(span // part):
+                text_block(g, r, 0, True)
+        if key_blocks > 1:
+            def more(p):
+                for g in heads:
+                    for r in range(span // part):
+                        text_block(g, r, p, False)
+            loop(1, (me * rows + rows - 1) // block_keys + 1, more)
+
     def image_on(j):
         i_in(j).wait_recv()
         i_mate(j).start()
 
+    text_heads(range(kv // 2))
     others(0, seen, image_on)
-    loop(0, seen, lambda j: t_mate_in(j).wait_recv())
-
-    span = group * rows
-    plane = 2 * inner * rows
-    q_pos = me * rows + lax.rem(lax.broadcasted_iota(jnp.int32, (span, 1), 0), rows)
-    factor = math.log2(math.e) / math.sqrt(HEAD_DIM)
-
-    def attend(g, keys, values, pos):
-        s = dot(qs[g], keys, 1, 1)
-        s = jnp.where(pos <= q_pos, s, NEG)
-        before = m_ref[g]
-        now = jnp.maximum(before, jnp.max(s, axis=1, keepdims=True))
-        shrink = jnp.exp2((before - now) * factor)
-        weight = jnp.exp2((s - now[:, 0:1]) * factor).astype(BF16)
-        both = jnp.concatenate([values, jnp.ones_like(values)], axis=1)
-        product = dot(weight, both, 1, 0)
-        acc_ref[g, :, :HEAD_DIM] = acc_ref[g, :, :HEAD_DIM] * shrink + product[:, :HEAD_DIM]
-        acc_ref[g, :, HEAD_DIM:] = acc_ref[g, :, HEAD_DIM:] * shrink + product[:, HEAD_DIM:]
-        m_ref[g] = now
-
-    m_ref[...] = jnp.full(m_ref.shape, NEG, F32)
-    acc_ref[...] = jnp.zeros_like(acc_ref)
-
-    def text_step(p):
-        at = pl.ds(pl.multiple_of(p * plane, plane), plane)
-        pos = pos_t[:, at]
-        for g in range(kv):
-            lo = g * HEAD_DIM
-            attend(g, tkv[at, lo:lo + HEAD_DIM], tkv[at, width + lo:width + lo + HEAD_DIM], pos)
-
-    loop(0, a + 1, text_step)
+    text_heads(range(kv // 2, kv))
 
     loop(0, seen, lambda j: i_mate_in(j).wait_recv())
     local = lax.broadcasted_iota(jnp.int32, (rows, SLOTS), 0)
@@ -295,18 +314,19 @@
     local = lax.broadcasted_iota(jnp.int32, (rows, width), 0)
     is_image = (local >= offset) & (local < offset + count)
     mine_slots = pl.ds(pl.multiple_of(core * SLOTS, SLOTS), SLOTS)
-    for part, (ref, text_ref) in enumerate(((ck_ref, tk_ref), (cv_ref, tv_ref))):
-        placed = dot(hot, img[part, chip, mine_slots, :], 1, 0)
+    for c, (ref, text_ref) in enumerate(((ck_ref, tk_ref), (cv_ref, tv_ref))):
+        placed = dot(hot, img[c, chip, mine_slots, :], 1, 0)
         ref[...] = jnp.where(is_image, placed, text_ref[...].astype(F32)).astype(BF16)
     for g in range(kv):
-        at = slice(g * HEAD_DIM, (g + 1) * HEAD_DIM)
-        keys = img[0, :, :, at].reshape(slots, HEAD_DIM)
-        values = img[1, :, :, at].reshape(slots, HEAD_DIM)
-        attend(g, keys, values, pos_i[...])
-        done = acc_ref[g, :, :HEAD_DIM] / acc_ref[g, :, HEAD_DIM:]
-        for h in range(group):
-            at = (g * group + h) * HEAD_DIM
-            out_ref[:, at:at + HEAD_DIM] = done[h * rows:(h + 1) * rows].astype(BF16)
+        lanes = slice(g * HEAD_DIM, (g + 1) * HEAD_DIM)
+        keys = img[0, :, :, lanes].reshape(slots, HEAD_DIM)
+        values = img[1, :, :, lanes].reshape(slots, HEAD_DIM)
+        for r in range(span // part):
+            now, summed, totals = attend(g, r, keys, values, pos_i[...], False)
+            done = (summed / totals).astype(BF16)
+            for h in range(part // rows):
+                at = (g * group + r * (part // rows) + h) * HEAD_DIM
+                out_ref[:, at:at + HEAD_DIM] = done[h * rows:(h + 1) * rows]
 
     loop(1, n, lambda d: meta_copy(d).wait_send())
     p1.wait_send()

time: 56.9 us -> 44.1 us (0.78)
  the two profiles are of different devices: /device:TPU:25 before, /device:TPU:29 now
where the time goes in v2:
time: 44.1 us; the launch traced here: 43.9 us
  Pallas kernels  39.9 us (90%)
  local copies, waits for them, and re-layouts  3.4 us (8%)
  between operations  0.65 us (1%)
    pallas_call x1, Pallas kernels, body(): pl.pallas_call(functools.partial(kernel, n, inner), out_shape=(jax.ShapeD...  39.9 us
    unnamed x7, local copies, waits for them, and re-layouts  3.4 us

profile of v2, /device:TPU:29, one launch (start us, length us, event | category | flops | bytes accessed | tf_op | source)
XLA Modules:
  0.0 43.9 jit_solution(6454777243036425146)
XLA Ops:
  0.6 39.9 %shard_map.94 = (bf16[64,4096]{1,0:T(8,128)(2,1)}, bf16[64,512]{1,0:T(8,128)(2,1)}, bf16[64,512]{1,0:T(8,128)(2,1)}) custom-call(bf16[64,4096]{1,0:T(8,128)(2,1)} %q_ref.1, bf16[64,512]{1,0:T(8,128)(2,1)} %tk_ref.1, bf16[64,512]{1,0:T(8,128)(2,1)} %tv_ref.1, bf16[512,256]{1,0:T(8,128)(2,1)} %feat_ref.1, bf16[512,1024]{1,0:T(8,128)(2,1)} %w_ref.1, ...), custom_call_target="tpu_custom_call" | custom-call | flops 1073741824 | bytes 1048576 | tf_op jit(solution)/shard_map/pallas_call | solution.py:357
  40.5 0.0 copy-start.1
  40.5 1.9 %copy.13 = bf16[64,4096]{1,0:T(8,128)(2,1)} copy(bf16[64,4096]{1,0:T(8,128)(2,1)} %get-tuple-element.6) | data formatting | bytes 1048576
  42.4 0.0 copy-done.1
  42.4 0.0 copy-start
  42.4 0.6 %copy.14 = bf16[64,512]{1,0:T(8,128)(2,1)} copy(bf16[64,512]{1,0:T(8,128)(2,1)S(1)} %copy-done.1) | data formatting | bytes 131072
  43.0 0.2 copy-done
  43.3 0.6 %copy.15 = bf16[64,512]{1,0:T(8,128)(2,1)} copy(bf16[64,512]{1,0:T(8,128)(2,1)S(1)} %copy-done) | data formatting | bytes 131072
Async XLA Ops:
  40.5 1.9 %copy-start.1 = (bf16[64,512]{1,0:T(8,128)(2,1)S(1)}, bf16[64,512]{1,0:T(8,128)(2,1)}, u32[]{:S(2)}) copy-start(bf16[64,512]{1,0:T(8,128)(2,1)} %get-tuple-element.7) | copy-start | bytes 196612
  42.4 0.9 %copy-start = (bf16[64,512]{1,0:T(8,128)(2,1)S(1)}, bf16[64,512]{1,0:T(8,128)(2,1)}, u32[]{:S(2)}) copy-start(bf16[64,512]{1,0:T(8,128)(2,1)} %get-tuple-element.8) | copy-start | bytes 196612

commit v3 on v2

--- a/solution.py
+++ b/solution.py
@@ -24,11 +24,11 @@
 
 def kernel(
     n, inner,
-    q_ref, tk_ref, tv_ref, feat_ref, w_ref, grid_ref, freq_ref,
+    q_hbm, tk_ref, tv_ref, feat_hbm, w_hbm, grid_ref, freq_ref,
     out_ref, ck_ref, cv_ref,
-    tkv, img, meta, mine, p1_src, p1_dst, p2_src, p2_dst, qs, pos_t, pos_i, m_ref, acc_ref,
-    meta_s, meta_r, p1_s, p1_r, p2_s, p2_r,
-    tz_s, ty_s, t_r, tm_s, tm_r, i_s, i_r, im_s, im_r,
+    q_ref, feat_ref, w_ref, load_s, tkv, img, info, info_sum, mine, p1_src, p1_dst, p2_src, p2_dst, qs, pos_t, pos_i, m_ref, acc_ref,
+    info_s, info_r, p1_s, p1_r, p2_s, p2_r,
+    tz_s, ty_s, t_r, tm_s, tm_r, i_s, is_s, i_r, im_s, im_r,
 ):
     chips = n // 2
     outer = chips // inner
@@ -54,13 +54,16 @@
             device_id={"ctx": target}, device_id_type=pl.DeviceIdType.MESH,
         )
 
+    loads = [pltpu.make_async_copy(src, dst, load_s.at[i]) for i, (src, dst) in enumerate(
+        ((feat_hbm, feat_ref), (w_hbm, w_ref), (q_hbm, q_ref)))]
+    for load in loads:
+        load.start()
+
     own = pl.ds(pl.multiple_of(me * rows, rows), rows)
     tkv[:, width:] = jnp.zeros((n * rows, width), BF16)
     tkv[own, :width] = tk_ref[...]
     tkv[own, width:] = tv_ref[...]
     offset, tall, wide = grid_ref[0, 0], grid_ref[0, 1], grid_ref[0, 2]
-    line = lax.broadcasted_iota(jnp.int32, (8, 128), 0)
-    meta[me] = jnp.where(line == 0, offset, jnp.where(line == 1, tall, wide))
     img[...] = jnp.zeros_like(img)
 
     barrier = pltpu.get_barrier_semaphore()
@@ -73,15 +76,15 @@
         shard = 2 * j + core
         return tkv.at[pl.ds(pl.multiple_of(shard * rows, rows), rows), :]
 
-    def meta_copy(d):
-        return copy(meta.at[me], meta.at[me], meta_s.at[d], meta_r.at[me], lax.rem(me + d, n))
-
-    def meta_in(j):
-        return copy(meta.at[j], meta.at[j], meta_s.at[0], meta_r.at[j], mate)
-
-    def up_copy(to):
-        return copy(block(chip), block(chip), tz_s.at[to], t_r.at[chip],
-                    2 * (to * inner + b) + core)
+    def info_copy(d):
+        return copy(info.at[me], info.at[me], info_s.at[d], info_r.at[me], lax.rem(me + d, n))
+
+    def info_in(j):
+        return copy(info.at[j], info.at[j], info_s.at[0], info_r.at[j], mate)
+
+    def up_copy(from_a):
+        j = from_a * inner + b
+        return copy(block(j), block(j), tz_s.at[from_a], t_r.at[j], me + 2 * inner)
 
     def side_copy(from_a, d):
         j = from_a * inner + b
@@ -99,34 +102,34 @@
         ref = tkv.at[pl.ds(pl.multiple_of(shard * rows, rows), rows), :]
         return copy(ref, ref, tm_s.at[j], tm_r.at[j], mate)
 
-    loop(1, n, lambda d: meta_copy(d).start())
-    loop(a + 1, outer, lambda to: up_copy(to).start())
+    @pl.when(a + 1 < outer)
+    def _():
+        up_copy(a).start()
+
     loop(1, inner, lambda d: side_copy(a, d).start())
+    t_mate(chip).start()
+
+    loads[0].wait()
+    wide_f = feat_ref[...].astype(F32)
+    power = jnp.sum(wide_f * wide_f, axis=0, keepdims=True)
+    line = lax.broadcasted_iota(jnp.int32, info.shape[1:], 0)
+    facts = jnp.where(line == 0, offset, jnp.where(line == 1, tall, wide)).astype(F32)
+    for i in range(slots // 128):
+        facts = jnp.where(line == 3 + i, power[:, i * 128:(i + 1) * 128], facts)
+    info[me] = facts
+    loop(1, n, lambda d: info_copy(d).start())
 
     half = lambda c: w_ref[:, pl.ds(pl.multiple_of(c * width, width), width)]
     features = feat_ref[...].T
-    p1_src[:, :width] = dot(features, half(1 - core), 1, 0).astype(BF16)
-    wide_f = features.astype(F32)
-    power = jnp.sum(wide_f * wide_f, axis=1, keepdims=True)
-    power = jnp.broadcast_to(power, (slots, 128))
-    lane_s = lax.broadcasted_iota(jnp.int32, (slots, 128), 1)
-
-    def split(x):
-        top = x.astype(BF16)
-        return jnp.where(lane_s < 64, top, (x - top.astype(F32)).astype(BF16))
-
-    p1_src[:, width:] = split(power)
+    loads[1].wait()
+    p1_src[...] = dot(features, half(1 - core), 1, 0).astype(BF16)
     p1 = copy(p1_src, p1_dst, p1_s, p1_r, mate)
     p1.start()
-    mine[:, :width] = dot(features, half(core), 1, 0)
-    mine[:, width:] = power
+    mine[...] = dot(features, half(core), 1, 0)
     p1.wait_recv()
-    mine[:, :width] = mine[:, :width] + p1_dst[:, :width].astype(F32)
-    other = p1_dst[:, width:].astype(F32)
-    power = power + other[:, 0:1] + other[:, 64:65]
-    mine[:, width:] = power
-    p2_src[:, :width] = mine[:, :width].astype(BF16)
-    p2_src[:, width:] = split(power)
+    both_cores = mine[...] + p1_dst[...].astype(F32)
+    mine[...] = both_cores
+    p2_src[...] = both_cores.astype(BF16)
 
     def p2_copy(d):
         j = lax.rem(chip + d, chips)
@@ -137,38 +140,41 @@
         return copy(p2_dst.at[j], p2_dst.at[j], p2_s.at[0], p2_r.at[j], mate)
 
     loop(1, chips, lambda d: p2_copy(d).start())
-    t_mate(chip).start()
-
+
+    def pass_on(i):
+        from_a = a - 1 - i
+        j = from_a * inner + b
+        t_in(j).wait_recv()
+
+        @pl.when(a + 1 < outer)
+        def _():
+            up_copy(from_a).start()
+
+        loop(1, inner, lambda d: side_copy(from_a, d).start())
+        t_mate(j).start()
+
+    early = jnp.minimum(a, 2)
+    loop(0, jnp.minimum(a, 1), pass_on)
+
+    loads[2].wait()
     for g in range(kv):
         for h in range(group):
             at = (g * group + h) * HEAD_DIM
             qs[g, h * rows:(h + 1) * rows, :] = q_ref[:, at:at + HEAD_DIM]
 
-    def meta_wait(d):
-        meta_in(lax.rem(me + d, n)).wait_recv()
-
-    loop(1, n, meta_wait)
-    lane_t = lax.broadcasted_iota(jnp.int32, pos_t.shape, 1)
-    lane_i = lax.broadcasted_iota(jnp.int32, pos_i.shape, 1)
-
-    def place(j, carry):
-        text, image = carry
-        o, t, w = meta[j, 0:1, 0:1], meta[j, 1:2, 0:1], meta[j, 2:3, 0:1]
-        begin = j * rows + o
-        dead = (lane_t >= begin) & (lane_t < begin + t * w)
-        k = lane_i - j * SLOTS
-        live = (k >= 0) & (k < t * w)
-        return jnp.where(dead, BIG, text), jnp.where(live, begin + k, image)
-
-    text, image = lax.fori_loop(0, n, place, (lane_t, jnp.full(pos_i.shape, BIG, jnp.int32)))
-    pos_t[...] = text
-    pos_i[...] = image
+    def gather_facts(d, total):
+        j = lax.rem(me + d, n)
+        info_in(j).wait_recv()
+        return total + info[j]
+
+    info_sum[...] = lax.fori_loop(1, n, gather_facts, info[me])
 
     row = lax.broadcasted_iota(jnp.int32, (pair, 128), 0)
     lane = lax.broadcasted_iota(jnp.int32, (pair, 128), 1)
     second = row >= SLOTS
     k = jnp.where(second, row - SLOTS, row)
-    pick = lambda i: jnp.where(second, meta[2 * chip + 1, i:i + 1, :], meta[2 * chip, i:i + 1, :])
+    pick = lambda i: jnp.where(
+        second, info[2 * chip + 1, i:i + 1, :], info[2 * chip, i:i + 1, :]).astype(jnp.int32)
     gw = pick(2)
     gy = jnp.zeros_like(k)
     for i in range(1, SLOTS // 2):
@@ -185,27 +191,19 @@
     sine = jnp.where(is_key, jnp.sin(angle), 0.0)
     sine = jnp.where(lane < HEAD_DIM // 2, -sine, sine)
 
-    def pass_on(i):
-        from_a = a - 1 - i
-        j = from_a * inner + b
-        t_in(j).wait_recv()
-        loop(1, inner, lambda d: side_copy(from_a, d).start())
-        t_mate(j).start()
-
-    loop(0, a, pass_on)
+    loop(jnp.minimum(a, 1), early, pass_on)
 
     mine_rows = pl.ds(pl.multiple_of(chip * pair, pair), pair)
 
-    def add(d, carry):
-        total, extra = carry
+    def add(d, total):
         src = lax.rem(chip + d, chips)
         p2_in(src).wait_recv()
-        return (total + p2_dst[src, :, :width].astype(F32),
-                extra + p2_dst[src, :, width:].astype(F32))
-
-    total, extra = lax.fori_loop(
-        1, chips, add, (mine[mine_rows, :width], jnp.zeros((pair, 128), F32)))
-    power = mine[mine_rows, width:] + extra[:, 0:1] + extra[:, 64:65]
+        return total + p2_dst[src].astype(F32)
+
+    total = lax.fori_loop(1, chips, add, mine[mine_rows, :])
+    squares = info_sum[pl.ds(3 + chip * pair // 128, 1), :]
+    squares = jnp.where(lane == lax.rem(chip * pair, 128) + row, squares, 0.0)
+    power = jnp.sum(squares, axis=1, keepdims=True)
     scale = lax.rsqrt(power / total_features + 1e-6)
     for h in range(kv):
         at = slice(h * HEAD_DIM, (h + 1) * HEAD_DIM)
@@ -213,8 +211,14 @@
         turned = jnp.concatenate([x[:, HEAD_DIM // 2:], x[:, :HEAD_DIM // 2]], axis=1)
         img[core, chip, :, at] = (x * cosine + turned * sine).astype(BF16)
 
-    def i_copy(j):
-        return copy(img.at[core, chip], img.at[core, chip], i_s.at[j], i_r.at[chip], 2 * j + core)
+    def i_copy(to_a):
+        return copy(img.at[core, chip], img.at[core, chip], i_s.at[to_a], i_r.at[chip],
+                    2 * (to_a * inner + b) + core)
+
+    def i_side(from_a, d):
+        j = from_a * inner + b
+        return copy(img.at[core, j], img.at[core, j], is_s.at[from_a * inner + d], i_r.at[j],
+                    2 * (a * inner + lax.rem(b + d, inner)) + core)
 
     def i_in(j):
         return copy(img.at[core, j], img.at[core, j], i_s.at[0], i_r.at[j], mate)
@@ -225,16 +229,11 @@
     def i_mate_in(j):
         return copy(img.at[1 - core, j], img.at[1 - core, j], im_s.at[j], im_r.at[j], mate)
 
-    def others(low, high, f):
-        def step(j):
-            @pl.when(j != chip)
-            def _():
-                f(j)
-        loop(low, high, step)
-
     seen = (a + 1) * inner
-    others(a * inner, chips, lambda j: i_copy(j).start())
+    loop(a + 1, outer, lambda to: i_copy(to).start())
+    loop(1, inner, lambda d: i_side(a, d).start())
     i_mate(chip).start()
+    loop(early, a, pass_on)
 
     def from_side(i):
         from_a = a - i
@@ -247,6 +246,22 @@
         loop(1, inner, step)
 
     loop(0, a + 1, from_side)
+
+    lane_t = lax.broadcasted_iota(jnp.int32, pos_t.shape, 1)
+    lane_i = lax.broadcasted_iota(jnp.int32, pos_i.shape, 1)
+
+    def place(j, carry):
+        text, image = carry
+        o, t, w = (info[j, i:i + 1, 0:1].astype(jnp.int32) for i in range(3))
+        begin = j * rows + o
+        dead = (lane_t >= begin) & (lane_t < begin + t * w)
+        k = lane_i - j * SLOTS
+        live = (k >= 0) & (k < t * w)
+        return jnp.where(dead, BIG, text), jnp.where(live, begin + k, image)
+
+    text, image = lax.fori_loop(0, n, place, (lane_t, jnp.full(pos_i.shape, BIG, jnp.int32)))
+    pos_t[...] = text
+    pos_i[...] = image
 
     loop(0, seen, lambda j: t_mate_in(j).wait_recv())
 
@@ -298,13 +313,25 @@
                         text_block(g, r, p, False)
             loop(1, (me * rows + rows - 1) // block_keys + 1, more)
 
-    def image_on(j):
+    def image_on(from_a):
+        j = from_a * inner + b
         i_in(j).wait_recv()
+        loop(1, inner, lambda d: i_side(from_a, d).start())
         i_mate(j).start()
 
-    text_heads(range(kv // 2))
-    others(0, seen, image_on)
-    text_heads(range(kv // 2, kv))
+    def image_from_side(from_a):
+        def step(d):
+            j = from_a * inner + lax.rem(b + d, inner)
+            i_in(j).wait_recv()
+            i_mate(j).start()
+
+        loop(1, inner, step)
+
+    text_heads(range(kv - 2))
+    loop(0, a, image_on)
+    text_heads(range(kv - 2, kv - 1))
+    loop(0, a + 1, image_from_side)
+    text_heads(range(kv - 1, kv))
 
     loop(0, seen, lambda j: i_mate_in(j).wait_recv())
     local = lax.broadcasted_iota(jnp.int32, (rows, SLOTS), 0)
@@ -328,13 +355,18 @@
                 at = (g * group + r * (part // rows) + h) * HEAD_DIM
                 out_ref[:, at:at + HEAD_DIM] = done[h * rows:(h + 1) * rows]
 
-    loop(1, n, lambda d: meta_copy(d).wait_send())
+    loop(1, n, lambda d: info_copy(d).wait_send())
     p1.wait_send()
     loop(1, chips, lambda d: p2_copy(d).wait_send())
-    loop(a + 1, outer, lambda to: up_copy(to).wait_send())
+
+    @pl.when(a + 1 < outer)
+    def _():
+        loop(0, a + 1, lambda f: up_copy(f).wait_send())
+
     loop(0, a + 1, lambda f: loop(1, inner, lambda d: side_copy(f, d).wait_send()))
+    loop(0, a + 1, lambda f: loop(1, inner, lambda d: i_side(f, d).wait_send()))
     loop(0, seen, lambda j: t_mate(j).wait_send())
-    others(a * inner, chips, lambda j: i_copy(j).wait_send())
+    loop(a + 1, outer, lambda to: i_copy(to).wait_send())
     loop(0, seen, lambda j: i_mate(j).wait_send())
 
 
@@ -354,6 +386,8 @@
     dma = pltpu.SemaphoreType.DMA
     vmem = pl.BlockSpec(memory_space=pltpu.VMEM)
     smem = pl.BlockSpec(memory_space=pltpu.SMEM)
+    hbm = pl.BlockSpec(memory_space=pl.ANY)
+    lines = -(-(3 + slots // 128) // 8) * 8
     return pl.pallas_call(
         functools.partial(kernel, n, inner),
         out_shape=(
@@ -361,17 +395,22 @@
             jax.ShapeDtypeStruct(text_keys.shape, BF16),
             jax.ShapeDtypeStruct(text_values.shape, BF16),
         ),
-        in_specs=[vmem] * 5 + [smem, vmem],
+        in_specs=[hbm, vmem, vmem, hbm, hbm, smem, vmem],
         out_specs=(vmem,) * 3,
         scratch_shapes=[
+            pltpu.VMEM(queries.shape, BF16),
+            pltpu.VMEM(image_features.shape, BF16),
+            pltpu.VMEM(kv_weight.shape, BF16),
+            dma((3,)),
             pltpu.VMEM((n * rows, 2 * width), BF16),
             pltpu.VMEM((2, chips, pair, width), BF16),
-            pltpu.VMEM((n, 8, 128), jnp.int32),
-            pltpu.VMEM((slots, width + 128), F32),
-            pltpu.VMEM((slots, width + 128), BF16),
-            pltpu.VMEM((slots, width + 128), BF16),
-            pltpu.VMEM((slots, width + 128), BF16),
-            pltpu.VMEM((chips, pair, width + 128), BF16),
+            pltpu.VMEM((n, lines, 128), F32),
+            pltpu.VMEM((lines, 128), F32),
+            pltpu.VMEM((slots, width), F32),
+            pltpu.VMEM((slots, width), BF16),
+            pltpu.VMEM((slots, width), BF16),
+            pltpu.VMEM((slots, width), BF16),
+            pltpu.VMEM((chips, pair, width), BF16),
             pltpu.VMEM((kv, span, HEAD_DIM), BF16),
             pltpu.VMEM((1, n * rows), jnp.int32),
             pltpu.VMEM((1, slots), jnp.int32),
@@ -379,7 +418,7 @@
             pltpu.VMEM((kv, span, 2 * HEAD_DIM), F32),
             dma((n,)), dma((n,)), dma, dma, dma((chips,)), dma((chips,)),
             dma((outer,)), dma((chips,)), dma((chips,)), dma((chips,)), dma((chips,)),
-            dma((chips,)), dma((chips,)), dma((chips,)), dma((chips,)),
+            dma((outer,)), dma((chips,)), dma((chips,)), dma((chips,)), dma((chips,)),
         ],
         compiler_params=pltpu.CompilerParams(
             collective_id=0, has_side_effects=True, vmem_limit_bytes=60 * 1024 * 1024

time: 44.1 us -> 45.1 us (1.023)
  the two profiles are of different devices: /device:TPU:29 before, /device:TPU:25 now
where the time goes in v3:
time: 45.1 us; the launch traced here: 44.9 us
  Pallas kernels  40.8 us (90%)
  local copies, waits for them, and re-layouts  3.4 us (8%)
  between operations  0.65 us (1%)
    pallas_call x1, Pallas kernels, body(): pl.pallas_call(functools.partial(kernel, n, inner), out_shape=(jax.ShapeD...  40.8 us
    unnamed x7, local copies, waits for them, and re-layouts  3.4 us

profile of v3, /device:TPU:25, one launch (start us, length us, event | category | flops | bytes accessed | tf_op | source)
XLA Modules:
  0.0 44.9 jit_solution(12316445996089639350)
XLA Ops:
  0.6 40.8 %shard_map.94 = (bf16[64,4096]{1,0:T(8,128)(2,1)}, bf16[64,512]{1,0:T(8,128)(2,1)}, bf16[64,512]{1,0:T(8,128)(2,1)}) custom-call(bf16[64,4096]{1,0:T(8,128)(2,1)} %q_hbm.1, bf16[64,512]{1,0:T(8,128)(2,1)} %tk_ref.1, bf16[64,512]{1,0:T(8,128)(2,1)} %tv_ref.1, bf16[512,256]{1,0:T(8,128)(2,1)} %feat_hbm.1, bf16[512,1024]{1,0:T(8,128)(2,1)} %w_hbm.1, ...), custom_call_target="tpu_custom_call" | custom-call | flops 1073741824 | bytes 1048576 | tf_op jit(solution)/shard_map/pallas_call | solution.py:391
  41.5 0.0 copy-start.1
  41.5 1.9 %copy.13 = bf16[64,4096]{1,0:T(8,128)(2,1)} copy(bf16[64,4096]{1,0:T(8,128)(2,1)} %get-tuple-element.6) | data formatting | bytes 1048576
  43.4 0.0 copy-done.1
  43.4 0.0 copy-start
  43.4 0.6 %copy.14 = bf16[64,512]{1,0:T(8,128)(2,1)} copy(bf16[64,512]{1,0:T(8,128)(2,1)S(1)} %copy-done.1) | data formatting | bytes 131072
  44.0 0.2 copy-done
  44.3 0.6 %copy.15 = bf16[64,512]{1,0:T(8,128)(2,1)} copy(bf16[64,512]{1,0:T(8,128)(2,1)S(1)} %copy-done) | data formatting | bytes 131072
Async XLA Ops:
  41.5 1.9 %copy-start.1 = (bf16[64,512]{1,0:T(8,128)(2,1)S(1)}, bf16[64,512]{1,0:T(8,128)(2,1)}, u32[]{:S(2)}) copy-start(bf16[64,512]{1,0:T(8,128)(2,1)} %get-tuple-element.7) | copy-start | bytes 196612
  43.4 0.9 %copy-start = (bf16[64,512]{1,0:T(8,128)(2,1)S(1)}, bf16[64,512]{1,0:T(8,128)(2,1)}, u32[]{:S(2)}) copy-start(bf16[64,512]{1,0:T(8,128)(2,1)} %get-tuple-element.8) | copy-start | bytes 196612

commit v4 on v3

--- a/solution.py
+++ b/solution.py
@@ -109,7 +109,15 @@
     loop(1, inner, lambda d: side_copy(a, d).start())
     t_mate(chip).start()
 
+    half = lambda c: w_ref[:, pl.ds(pl.multiple_of(c * width, width), width)]
     loads[0].wait()
+    features = feat_ref[...].T
+    loads[1].wait()
+    p1_src[...] = dot(features, half(1 - core), 1, 0).astype(BF16)
+    p1 = copy(p1_src, p1_dst, p1_s, p1_r, mate)
+    p1.start()
+    mine[...] = dot(features, half(core), 1, 0)
+
     wide_f = feat_ref[...].astype(F32)
     power = jnp.sum(wide_f * wide_f, axis=0, keepdims=True)
     line = lax.broadcasted_iota(jnp.int32, info.shape[1:], 0)
@@ -119,18 +127,25 @@
     info[me] = facts
     loop(1, n, lambda d: info_copy(d).start())
 
-    half = lambda c: w_ref[:, pl.ds(pl.multiple_of(c * width, width), width)]
-    features = feat_ref[...].T
-    loads[1].wait()
-    p1_src[...] = dot(features, half(1 - core), 1, 0).astype(BF16)
-    p1 = copy(p1_src, p1_dst, p1_s, p1_r, mate)
-    p1.start()
-    mine[...] = dot(features, half(core), 1, 0)
     p1.wait_recv()
     both_cores = mine[...] + p1_dst[...].astype(F32)
     mine[...] = both_cores
     p2_src[...] = both_cores.astype(BF16)
 
+    def pass_on(i):
+        from_a = a - 1 - i
+        j = from_a * inner + b
+        t_in(j).wait_recv()
+
+        @pl.when(a + 1 < outer)
+        def _():
+            up_copy(from_a).start()
+
+        loop(1, inner, lambda d: side_copy(from_a, d).start())
+        t_mate(j).start()
+
+    first_on = jnp.minimum(a, 1)
+
     def p2_copy(d):
         j = lax.rem(chip + d, chips)
         return copy(p2_src.at[pl.ds(pl.multiple_of(j * pair, pair), pair), :], p2_dst.at[chip],
@@ -139,22 +154,8 @@
     def p2_in(j):
         return copy(p2_dst.at[j], p2_dst.at[j], p2_s.at[0], p2_r.at[j], mate)
 
+    loop(0, first_on, pass_on)
     loop(1, chips, lambda d: p2_copy(d).start())
-
-    def pass_on(i):
-        from_a = a - 1 - i
-        j = from_a * inner + b
-        t_in(j).wait_recv()
-
-        @pl.when(a + 1 < outer)
-        def _():
-            up_copy(from_a).start()
-
-        loop(1, inner, lambda d: side_copy(from_a, d).start())
-        t_mate(j).start()
-
-    early = jnp.minimum(a, 2)
-    loop(0, jnp.minimum(a, 1), pass_on)
 
     loads[2].wait()
     for g in range(kv):
@@ -191,7 +192,7 @@
     sine = jnp.where(is_key, jnp.sin(angle), 0.0)
     sine = jnp.where(lane < HEAD_DIM // 2, -sine, sine)
 
-    loop(jnp.minimum(a, 1), early, pass_on)
+    loop(first_on, a, pass_on)
 
     mine_rows = pl.ds(pl.multiple_of(chip * pair, pair), pair)
 
@@ -233,19 +234,13 @@
     loop(a + 1, outer, lambda to: i_copy(to).start())
     loop(1, inner, lambda d: i_side(a, d).start())
     i_mate(chip).start()
-    loop(early, a, pass_on)
-
-    def from_side(i):
-        from_a = a - i
-
+    def from_side(from_a):
         def step(d):
             j = from_a * inner + lax.rem(b + d, inner)
             t_in(j).wait_recv()
             t_mate(j).start()
 
         loop(1, inner, step)
-
-    loop(0, a + 1, from_side)
 
     lane_t = lax.broadcasted_iota(jnp.int32, pos_t.shape, 1)
     lane_i = lax.broadcasted_iota(jnp.int32, pos_i.shape, 1)
@@ -263,12 +258,12 @@
     pos_t[...] = text
     pos_i[...] = image
 
-    loop(0, seen, lambda j: t_mate_in(j).wait_recv())
-
     span = group * rows
     part = math.gcd(span, 256)
-    block_keys = math.gcd(n * rows, 1024)
-    key_blocks = n * rows // block_keys
+    plane = 2 * inner * rows
+    block_keys = max(plane, math.gcd(n * rows, 512))
+    planes = block_keys // plane
+    last = a // planes
     factor = math.log2(math.e) / math.sqrt(HEAD_DIM)
     q_pos = me * rows + lax.rem(lax.broadcasted_iota(jnp.int32, (part, 1), 0), rows)
 
@@ -302,16 +297,15 @@
         acc_ref[g, at, :HEAD_DIM] = summed
         acc_ref[g, at, HEAD_DIM:] = totals
 
-    def text_heads(heads):
+    def text_heads(heads, p, first):
         for g in heads:
             for r in range(span // part):
-                text_block(g, r, 0, True)
-        if key_blocks > 1:
-            def more(p):
-                for g in heads:
-                    for r in range(span // part):
-                        text_block(g, r, p, False)
-            loop(1, (me * rows + rows - 1) // block_keys + 1, more)
+                text_block(g, r, p, first)
+
+    def text_wait(p):
+        low = p * planes * inner
+        high = jnp.minimum(seen, low + planes * inner)
+        loop(low, high, lambda j: t_mate_in(j).wait_recv())
 
     def image_on(from_a):
         j = from_a * inner + b
@@ -327,11 +321,37 @@
 
         loop(1, inner, step)
 
-    text_heads(range(kv - 2))
-    loop(0, a, image_on)
-    text_heads(range(kv - 2, kv - 1))
-    loop(0, a + 1, image_from_side)
-    text_heads(range(kv - 1, kv))
+    def images_on():
+        loop(0, a, image_on)
+
+    def images_from_side():
+        loop(0, a + 1, image_from_side)
+
+    low = last * planes
+    loop(0, a + 1 - low, lambda i: from_side(a - i))
+    text_wait(last)
+    text_heads(range(kv // 2), last, True)
+    loop(0, low, lambda i: from_side(low - 1 - i))
+    text_heads(range(kv // 2, kv - 1), last, True)
+    images_on()
+    text_heads(range(kv - 1, kv), last, True)
+
+    def more(i):
+        p = last - 1 - i
+        text_wait(p)
+        text_heads(range(kv // 2), p, False)
+
+        @pl.when(p == 0)
+        def _():
+            images_from_side()
+
+        text_heads(range(kv // 2, kv), p, False)
+
+    loop(0, last, more)
+
+    @pl.when(last == 0)
+    def _():
+        images_from_side()
 
     loop(0, seen, lambda j: i_mate_in(j).wait_recv())
     local = lax.broadcasted_iota(jnp.int32, (rows, SLOTS), 0)

time: 45.1 us -> 40.6 us (0.900)
  Pallas kernels: 40.8 us -> 36.3 us
    pallas_call x1, Pallas kernels: 40.8 us -> 36.3 us  [body(): pl.pallas_call(functools.partial(kernel, n, inner), out_shape=(jax.ShapeD...]
where the time goes in v4:
time: 40.6 us; the launch traced here: 40.4 us
  Pallas kernels  36.3 us (89%)
  local copies, waits for them, and re-layouts  3.4 us (8%)
  between operations  0.65 us (2%)
    pallas_call x1, Pallas kernels, body(): pl.pallas_call(functools.partial(kernel, n, inner), out_shape=(jax.ShapeD...  36.3 us
    unnamed x7, local copies, waits for them, and re-layouts  3.4 us

profile of v4, /device:TPU:25, one launch (start us, length us, event | category | flops | bytes accessed | tf_op | source)
XLA Modules:
  0.0 40.4 jit_solution(17143211914941532165)
XLA Ops:
  0.6 36.3 %shard_map.94 = (bf16[64,4096]{1,0:T(8,128)(2,1)}, bf16[64,512]{1,0:T(8,128)(2,1)}, bf16[64,512]{1,0:T(8,128)(2,1)}) custom-call(bf16[64,4096]{1,0:T(8,128)(2,1)} %q_hbm.1, bf16[64,512]{1,0:T(8,128)(2,1)} %tk_ref.1, bf16[64,512]{1,0:T(8,128)(2,1)} %tv_ref.1, bf16[512,256]{1,0:T(8,128)(2,1)} %feat_hbm.1, bf16[512,1024]{1,0:T(8,128)(2,1)} %w_hbm.1, ...), custom_call_target="tpu_custom_call" | custom-call | flops 1073741824 | bytes 1048576 | tf_op jit(solution)/shard_map/pallas_call | solution.py:411
  37.0 0.0 copy-start.1
  37.0 1.9 %copy.13 = bf16[64,4096]{1,0:T(8,128)(2,1)} copy(bf16[64,4096]{1,0:T(8,128)(2,1)} %get-tuple-element.6) | data formatting | bytes 1048576
  38.9 0.0 copy-done.1
  38.9 0.0 copy-start
  38.9 0.6 %copy.14 = bf16[64,512]{1,0:T(8,128)(2,1)} copy(bf16[64,512]{1,0:T(8,128)(2,1)S(1)} %copy-done.1) | data formatting | bytes 131072
  39.5 0.2 copy-done
  39.8 0.6 %copy.15 = bf16[64,512]{1,0:T(8,128)(2,1)} copy(bf16[64,512]{1,0:T(8,128)(2,1)S(1)} %copy-done) | data formatting | bytes 131072
Async XLA Ops:
  37.0 1.9 %copy-start.1 = (bf16[64,512]{1,0:T(8,128)(2,1)S(1)}, bf16[64,512]{1,0:T(8,128)(2,1)}, u32[]{:S(2)}) copy-start(bf16[64,512]{1,0:T(8,128)(2,1)} %get-tuple-element.7) | copy-start | bytes 196612
  38.9 0.9 %copy-start = (bf16[64,512]{1,0:T(8,128)(2,1)S(1)}, bf16[64,512]{1,0:T(8,128)(2,1)}, u32[]{:S(2)}) copy-start(bf16[64,512]{1,0:T(8,128)(2,1)} %get-tuple-element.8) | copy-start | bytes 196612

commit v5 on v4

--- a/solution.py
+++ b/solution.py
@@ -26,8 +26,8 @@
     n, inner,
     q_hbm, tk_ref, tv_ref, feat_hbm, w_hbm, grid_ref, freq_ref,
     out_ref, ck_ref, cv_ref,
-    q_ref, feat_ref, w_ref, load_s, tkv, img, info, info_sum, mine, p1_src, p1_dst, p2_src, p2_dst, qs, pos_t, pos_i, m_ref, acc_ref,
-    info_s, info_r, p1_s, p1_r, p2_s, p2_r,
+    q_ref, feat_ref, w_ref, load_s, tkv, img, info, info_sum, mine, p1_src, p1_dst, p2_src, p2_dst, p3_src, p3_dst, qs, pos_t, pos_i, m_ref, acc_ref,
+    info_s, info_r, p1_s, p1_r, p2_s, p2_r, p3_s, p3_r,
     tz_s, ty_s, t_r, tm_s, tm_r, i_s, is_s, i_r, im_s, im_r,
 ):
     chips = n // 2
@@ -130,7 +130,9 @@
     p1.wait_recv()
     both_cores = mine[...] + p1_dst[...].astype(F32)
     mine[...] = both_cores
-    p2_src[...] = both_cores.astype(BF16)
+    for j in range(chips):
+        to = (j % inner * outer + j // inner) * pair
+        p2_src[to:to + pair, :] = both_cores[j * pair:(j + 1) * pair].astype(BF16)
 
     def pass_on(i):
         from_a = a - 1 - i
@@ -146,16 +148,42 @@
 
     first_on = jnp.minimum(a, 1)
 
+    column = outer * pair
+
     def p2_copy(d):
-        j = lax.rem(chip + d, chips)
-        return copy(p2_src.at[pl.ds(pl.multiple_of(j * pair, pair), pair), :], p2_dst.at[chip],
-                    p2_s.at[d], p2_r.at[chip], 2 * j + core)
+        to_b = lax.rem(b + d, inner)
+        return copy(p2_src.at[pl.ds(pl.multiple_of(to_b * column, column), column), :],
+                    p2_dst.at[b], p2_s.at[d], p2_r.at[b], 2 * (a * inner + to_b) + core)
 
     def p2_in(j):
         return copy(p2_dst.at[j], p2_dst.at[j], p2_s.at[0], p2_r.at[j], mate)
 
+    def p3_copy(d):
+        to_a = lax.rem(a + d, outer)
+        return copy(p3_src.at[to_a], p3_dst.at[a], p3_s.at[d], p3_r.at[a],
+                    2 * (to_a * inner + b) + core)
+
+    def p3_in(j):
+        return copy(p3_dst.at[j], p3_dst.at[j], p3_s.at[0], p3_r.at[j], mate)
+
+    def column_sum(of_a):
+        at = pl.ds(pl.multiple_of((of_a * inner + b) * pair, pair), pair)
+        total = mine[at, :]
+        at = pl.ds(pl.multiple_of(of_a * pair, pair), pair)
+        return lax.fori_loop(
+            1, inner,
+            lambda d, x: x + p2_dst[lax.rem(b + d, inner), at, :].astype(F32), total)
+
+    loop(1, inner, lambda d: p2_copy(d).start())
     loop(0, first_on, pass_on)
-    loop(1, chips, lambda d: p2_copy(d).start())
+    loop(1, inner, lambda d: p2_in(lax.rem(b + d, inner)).wait_recv())
+
+    def send_sum(d):
+        to_a = lax.rem(a + d, outer)
+        p3_src[to_a] = column_sum(to_a).astype(BF16)
+        p3_copy(d).start()
+
+    loop(1, outer, send_sum)
 
     loads[2].wait()
     for g in range(kv):
@@ -194,14 +222,33 @@
 
     loop(first_on, a, pass_on)
 
-    mine_rows = pl.ds(pl.multiple_of(chip * pair, pair), pair)
+    lane_t = lax.broadcasted_iota(jnp.int32, pos_t.shape, 1)
+    lane_i = lax.broadcasted_iota(jnp.int32, pos_i.shape, 1)
+    shard_t = lane_t // rows
+    shard_i = lane_i // SLOTS
+
+    def place(j, carry):
+        text, image = carry
+        code = info[j, 0:1, :] * 64.0 + info[j, 1:2, :] * info[j, 2:3, :]
+        spread = lambda x: jnp.concatenate([code] * (x.shape[1] // 128), axis=1)
+        return (jnp.where(shard_t == j, spread(text), text),
+                jnp.where(shard_i == j, spread(image), image))
+
+    text, image = lax.fori_loop(
+        0, n, place, (jnp.zeros(pos_t.shape, F32), jnp.zeros(pos_i.shape, F32)))
+    text, image = text.astype(jnp.int32), image.astype(jnp.int32)
+    within = lane_t - shard_t * rows - text // 64
+    pos_t[...] = jnp.where((within >= 0) & (within < text % 64), BIG, lane_t)
+    within = lane_i - shard_i * SLOTS
+    pos_i[...] = jnp.where(
+        within < image % 64, shard_i * rows + image // 64 + within, BIG)
 
     def add(d, total):
-        src = lax.rem(chip + d, chips)
-        p2_in(src).wait_recv()
-        return total + p2_dst[src].astype(F32)
-
-    total = lax.fori_loop(1, chips, add, mine[mine_rows, :])
+        src = lax.rem(a + d, outer)
+        p3_in(src).wait_recv()
+        return total + p3_dst[src].astype(F32)
+
+    total = lax.fori_loop(1, outer, add, column_sum(a))
     squares = info_sum[pl.ds(3 + chip * pair // 128, 1), :]
     squares = jnp.where(lane == lax.rem(chip * pair, 128) + row, squares, 0.0)
     power = jnp.sum(squares, axis=1, keepdims=True)
@@ -241,22 +288,6 @@
             t_mate(j).start()
 
         loop(1, inner, step)
-
-    lane_t = lax.broadcasted_iota(jnp.int32, pos_t.shape, 1)
-    lane_i = lax.broadcasted_iota(jnp.int32, pos_i.shape, 1)
-
-    def place(j, carry):
-        text, image = carry
-        o, t, w = (info[j, i:i + 1, 0:1].astype(jnp.int32) for i in range(3))
-        begin = j * rows + o
-        dead = (lane_t >= begin) & (lane_t < begin + t * w)
-        k = lane_i - j * SLOTS
-        live = (k >= 0) & (k < t * w)
-        return jnp.where(dead, BIG, text), jnp.where(live, begin + k, image)
-
-    text, image = lax.fori_loop(0, n, place, (lane_t, jnp.full(pos_i.shape, BIG, jnp.int32)))
-    pos_t[...] = text
-    pos_i[...] = image
 
     span = group * rows
     part = math.gcd(span, 256)
@@ -377,7 +408,8 @@
 
     loop(1, n, lambda d: info_copy(d).wait_send())
     p1.wait_send()
-    loop(1, chips, lambda d: p2_copy(d).wait_send())
+    loop(1, inner, lambda d: p2_copy(d).wait_send())
+    loop(1, outer, lambda d: p3_copy(d).wait_send())
 
     @pl.when(a + 1 < outer)
     def _():
@@ -430,13 +462,15 @@
             pltpu.VMEM((slots, width), BF16),
             pltpu.VMEM((slots, width), BF16),
             pltpu.VMEM((slots, width), BF16),
-            pltpu.VMEM((chips, pair, width), BF16),
+            pltpu.VMEM((inner, outer * pair, width), BF16),
+            pltpu.VMEM((outer, pair, width), BF16),
+            pltpu.VMEM((outer, pair, width), BF16),
             pltpu.VMEM((kv, span, HEAD_DIM), BF16),
             pltpu.VMEM((1, n * rows), jnp.int32),
             pltpu.VMEM((1, slots), jnp.int32),
             pltpu.VMEM((kv, span, HEAD_DIM), F32),
             pltpu.VMEM((kv, span, 2 * HEAD_DIM), F32),
-            dma((n,)), dma((n,)), dma, dma, dma((chips,)), dma((chips,)),
+            dma((n,)), dma((n,)), dma, dma, dma((inner,)), dma((inner,)), dma((outer,)), dma((outer,)),
             dma((outer,)), dma((chips,)), dma((chips,)), dma((chips,)), dma((chips,)),
             dma((outer,)), dma((chips,)), dma((chips,)), dma((chips,)), dma((chips,)),
         ],

time: 40.6 us -> 36.9 us (0.909)
  Pallas kernels: 36.3 us -> 32.7 us
    pallas_call x1, Pallas kernels: 36.3 us -> 32.7 us  [body(): pl.pallas_call(functools.partial(kernel, n, inner), out_shape=(jax.ShapeD...]
where the time goes in v5:
time: 36.9 us; the launch traced here: 36.7 us
  Pallas kernels  32.7 us (89%)
  local copies, waits for them, and re-layouts  3.4 us (9%)
  between operations  0.65 us (2%)
    pallas_call x1, Pallas kernels, body(): pl.pallas_call(functools.partial(kernel, n, inner), out_shape=(jax.ShapeD...  32.7 us
    unnamed x7, local copies, waits for them, and re-layouts  3.4 us

profile of v5, /device:TPU:25, one launch (start us, length us, event | category | flops | bytes accessed | tf_op | source)
XLA Modules:
  0.0 36.7 jit_solution(16311279110514867269)
XLA Ops:
  0.6 32.7 %shard_map.94 = (bf16[64,4096]{1,0:T(8,128)(2,1)}, bf16[64,512]{1,0:T(8,128)(2,1)}, bf16[64,512]{1,0:T(8,128)(2,1)}) custom-call(bf16[64,4096]{1,0:T(8,128)(2,1)} %q_hbm.1, bf16[64,512]{1,0:T(8,128)(2,1)} %tk_ref.1, bf16[64,512]{1,0:T(8,128)(2,1)} %tv_ref.1, bf16[512,256]{1,0:T(8,128)(2,1)} %feat_hbm.1, bf16[512,1024]{1,0:T(8,128)(2,1)} %w_hbm.1, ...), custom_call_target="tpu_custom_call" | custom-call | flops 1073741824 | bytes 1048576 | tf_op jit(solution)/shard_map/pallas_call | solution.py:443
  33.3 0.0 copy-start.1
  33.3 1.9 %copy.13 = bf16[64,4096]{1,0:T(8,128)(2,1)} copy(bf16[64,4096]{1,0:T(8,128)(2,1)} %get-tuple-element.6) | data formatting | bytes 1048576
  35.2 0.0 copy-done.1
  35.2 0.0 copy-start
  35.2 0.6 %copy.14 = bf16[64,512]{1,0:T(8,128)(2,1)} copy(bf16[64,512]{1,0:T(8,128)(2,1)S(1)} %copy-done.1) | data formatting | bytes 131072
  35.8 0.2 copy-done
  36.1 0.6 %copy.15 = bf16[64,512]{1,0:T(8,128)(2,1)} copy(bf16[64,512]{1,0:T(8,128)(2,1)S(1)} %copy-done) | data formatting | bytes 131072
Async XLA Ops:
  33.3 1.9 %copy-start.1 = (bf16[64,512]{1,0:T(8,128)(2,1)S(1)}, bf16[64,512]{1,0:T(8,128)(2,1)}, u32[]{:S(2)}) copy-start(bf16[64,512]{1,0:T(8,128)(2,1)} %get-tuple-element.7) | copy-start | bytes 196612
  35.2 0.9 %copy-start = (bf16[64,512]{1,0:T(8,128)(2,1)S(1)}, bf16[64,512]{1,0:T(8,128)(2,1)}, u32[]{:S(2)}) copy-start(bf16[64,512]{1,0:T(8,128)(2,1)} %get-tuple-element.8) | copy-start | bytes 196612

commit v6 on v5

--- a/solution.py
+++ b/solution.py
@@ -118,6 +118,56 @@
     p1.start()
     mine[...] = dot(features, half(core), 1, 0)
 
+    p1.wait_recv()
+    both_cores = mine[...] + p1_dst[...].astype(F32)
+    mine[...] = both_cores
+    for j in range(chips):
+        to = (j % inner * outer + j // inner) * pair
+        p2_src[to:to + pair, :] = both_cores[j * pair:(j + 1) * pair].astype(BF16)
+
+    def pass_on(i):
+        from_a = a - 1 - i
+        j = from_a * inner + b
+        t_in(j).wait_recv()
+
+        @pl.when(a + 1 < outer)
+        def _():
+            up_copy(from_a).start()
+
+        loop(1, inner, lambda d: side_copy(from_a, d).start())
+        t_mate(j).start()
+
+    first_on = jnp.minimum(a, 1)
+
+    column = outer * pair
+
+    def p2_copy(d):
+        to_b = lax.rem(b + d, inner)
+        return copy(p2_src.at[pl.ds(pl.multiple_of(to_b * column, column), column), :],
+                    p2_dst.at[b], p2_s.at[d], p2_r.at[b], 2 * (a * inner + to_b) + core)
+
+    def p2_in(j):
+        return copy(p2_dst.at[j], p2_dst.at[j], p2_s.at[0], p2_r.at[j], mate)
+
+    def p3_copy(d):
+        to_a = lax.rem(a + d, outer)
+        return copy(p3_src.at[to_a], p3_dst.at[a], p3_s.at[d], p3_r.at[a],
+                    2 * (to_a * inner + b) + core)
+
+    def p3_in(j):
+        return copy(p3_dst.at[j], p3_dst.at[j], p3_s.at[0], p3_r.at[j], mate)
+
+    def column_sum(of_a):
+        at = pl.ds(pl.multiple_of((of_a * inner + b) * pair, pair), pair)
+        total = mine[at, :]
+        at = pl.ds(pl.multiple_of(of_a * pair, pair), pair)
+        return lax.fori_loop(
+            1, inner,
+            lambda d, x: x + p2_dst[lax.rem(b + d, inner), at, :].astype(F32), total)
+
+    loop(1, inner, lambda d: p2_copy(d).start())
+    loop(0, first_on, pass_on)
+
     wide_f = feat_ref[...].astype(F32)
     power = jnp.sum(wide_f * wide_f, axis=0, keepdims=True)
     line = lax.broadcasted_iota(jnp.int32, info.shape[1:], 0)
@@ -127,55 +177,6 @@
     info[me] = facts
     loop(1, n, lambda d: info_copy(d).start())
 
-    p1.wait_recv()
-    both_cores = mine[...] + p1_dst[...].astype(F32)
-    mine[...] = both_cores
-    for j in range(chips):
-        to = (j % inner * outer + j // inner) * pair
-        p2_src[to:to + pair, :] = both_cores[j * pair:(j + 1) * pair].astype(BF16)
-
-    def pass_on(i):
-        from_a = a - 1 - i
-        j = from_a * inner + b
-        t_in(j).wait_recv()
-
-        @pl.when(a + 1 < outer)
-        def _():
-            up_copy(from_a).start()
-
-        loop(1, inner, lambda d: side_copy(from_a, d).start())
-        t_mate(j).start()
-
-    first_on = jnp.minimum(a, 1)
-
-    column = outer * pair
-
-    def p2_copy(d):
-        to_b = lax.rem(b + d, inner)
-        return copy(p2_src.at[pl.ds(pl.multiple_of(to_b * column, column), column), :],
-                    p2_dst.at[b], p2_s.at[d], p2_r.at[b], 2 * (a * inner + to_b) + core)
-
-    def p2_in(j):
-        return copy(p2_dst.at[j], p2_dst.at[j], p2_s.at[0], p2_r.at[j], mate)
-
-    def p3_copy(d):
-        to_a = lax.rem(a + d, outer)
-        return copy(p3_src.at[to_a], p3_dst.at[a], p3_s.at[d], p3_r.at[a],
-                    2 * (to_a * inner + b) + core)
-
-    def p3_in(j):
-        return copy(p3_dst.at[j], p3_dst.at[j], p3_s.at[0], p3_r.at[j], mate)
-
-    def column_sum(of_a):
-        at = pl.ds(pl.multiple_of((of_a * inner + b) * pair, pair), pair)
-        total = mine[at, :]
-        at = pl.ds(pl.multiple_of(of_a * pair, pair), pair)
-        return lax.fori_loop(
-            1, inner,
-            lambda d, x: x + p2_dst[lax.rem(b + d, inner), at, :].astype(F32), total)
-
-    loop(1, inner, lambda d: p2_copy(d).start())
-    loop(0, first_on, pass_on)
     loop(1, inner, lambda d: p2_in(lax.rem(b + d, inner)).wait_recv())
 
     def send_sum(d):

time: 36.9 us -> 40.1 us (1.087)
  Pallas kernels: 32.7 us -> 35.8 us
    pallas_call x1, Pallas kernels: 32.7 us -> 35.8 us  [body(): pl.pallas_call(functools.partial(kernel, n, inner), out_shape=(jax.ShapeD...]
where the time goes in v6:
time: 40.1 us; the launch traced here: 39.9 us
  Pallas kernels  35.8 us (89%)
  local copies, waits for them, and re-layouts  3.4 us (8%)
  between operations  0.65 us (2%)
    pallas_call x1, Pallas kernels, body(): pl.pallas_call(functools.partial(kernel, n, inner), out_shape=(jax.ShapeD...  35.8 us
    unnamed x7, local copies, waits for them, and re-layouts  3.4 us

profile of v6, /device:TPU:25, one launch (start us, length us, event | category | flops | bytes accessed | tf_op | source)
XLA Modules:
  0.0 39.9 jit_solution(17000129028550269244)
XLA Ops:
  0.6 35.8 %shard_map.94 = (bf16[64,4096]{1,0:T(8,128)(2,1)}, bf16[64,512]{1,0:T(8,128)(2,1)}, bf16[64,512]{1,0:T(8,128)(2,1)}) custom-call(bf16[64,4096]{1,0:T(8,128)(2,1)} %q_hbm.1, bf16[64,512]{1,0:T(8,128)(2,1)} %tk_ref.1, bf16[64,512]{1,0:T(8,128)(2,1)} %tv_ref.1, bf16[512,256]{1,0:T(8,128)(2,1)} %feat_hbm.1, bf16[512,1024]{1,0:T(8,128)(2,1)} %w_hbm.1, ...), custom_call_target="tpu_custom_call" | custom-call | flops 1073741824 | bytes 1048576 | tf_op jit(solution)/shard_map/pallas_call | solution.py:444
  36.5 0.0 copy-start.1
  36.5 1.9 %copy.13 = bf16[64,4096]{1,0:T(8,128)(2,1)} copy(bf16[64,4096]{1,0:T(8,128)(2,1)} %get-tuple-element.6) | data formatting | bytes 1048576
  38.4 0.0 copy-done.1
  38.4 0.0 copy-start
  38.4 0.6 %copy.14 = bf16[64,512]{1,0:T(8,128)(2,1)} copy(bf16[64,512]{1,0:T(8,128)(2,1)S(1)} %copy-done.1) | data formatting | bytes 131072
  39.0 0.2 copy-done
  39.3 0.6 %copy.15 = bf16[64,512]{1,0:T(8,128)(2,1)} copy(bf16[64,512]{1,0:T(8,128)(2,1)S(1)} %copy-done) | data formatting | bytes 131072
Async XLA Ops:
  36.5 1.9 %copy-start.1 = (bf16[64,512]{1,0:T(8,128)(2,1)S(1)}, bf16[64,512]{1,0:T(8,128)(2,1)}, u32[]{:S(2)}) copy-start(bf16[64,512]{1,0:T(8,128)(2,1)} %get-tuple-element.7) | copy-start | bytes 196612
  38.4 0.9 %copy-start = (bf16[64,512]{1,0:T(8,128)(2,1)S(1)}, bf16[64,512]{1,0:T(8,128)(2,1)}, u32[]{:S(2)}) copy-start(bf16[64,512]{1,0:T(8,128)(2,1)} %get-tuple-element.8) | copy-start | bytes 196612
